TPU v7x, 512 devices: a whole 4x4x16 slice. The times are simulated.
512 devices in a mesh: dom: 64 (over z, y_hi, core), feat: 8 (over x, y_lo).
Axes of the slice: x: 4, y: 4 (y_hi: 2, y_lo: 2; y = y_hi * 2 + y_lo), z: 16, core: 2. Of those that a mesh axis runs over, the one named last changes fastest.
Arguments:
- node_features: bfloat16 [65536, 128], P('dom'), may hold values from -6 to 6
- weight: bfloat16 [128, 256], P(None, 'feat'), may hold values from -0.5 to 0.5
- bias: float32 [256], P('feat'), may hold values from -3 to 3
- tile_values: bfloat16 [6144, 128, 128], P('dom')
- tile_src: int32 [6144], P('dom'), may hold values from 0 to 7
- tile_dst: int32 [6144], P('dom'), may hold values from 0 to 31, as said below
- tile_counts: int32 [64], P('dom'), may hold values from 4 to 96
- out_grad: bfloat16 [65536, 256], P('dom', 'feat'), may hold values from -6 to 6
Outputs:
- output: bfloat16 [65536, 256], P('dom', 'feat')
- weight_grad: float32 [128, 256], P(None, 'feat')
- bias_grad: float32 [256], P('feat')
- input_grad: bfloat16 [65536, 128], P('dom', 'feat')
Inputs may be any that keep to these rules, and one draw needn't show every extreme that they name: The partition offset tile_dst[k] // 8 of slot k of a partition equals k mod 4.
All inputs are finite; a program needn't handle non-finite values.
Results may differ from a plain program's by a relative error of at most 0.0075.
Values may be sent and summed in bfloat16 or wider, within the bound.
A program may use at most 64 MiB of HBM per device.

v0:
```python
import jax
import jax.numpy as jnp
from jax import lax
from jax.sharding import PartitionSpec as P

BLOCK = 128
REACH = 4


def passed_along(block, axis, distance):
    devices = range(lax.axis_size(axis))
    route = [((i - distance) % len(devices), i) for i in devices]
    return lax.ppermute(block, axis, route)


def shards(node_features, weight, bias, tile_values, tile_src, tile_dst, tile_counts, out_grad):
    node_rows = node_features.shape[0]
    blocks_dev = node_rows // BLOCK
    width_dev = weight.shape[1]
    capacity = tile_values.shape[0]
    live = jnp.arange(capacity, dtype=jnp.int32) < tile_counts[0]
    dst_segments = REACH * blocks_dev
    dst_ids = jnp.where(live, tile_dst, dst_segments)
    src_ids = jnp.where(live, tile_src, blocks_dev)
    projected = jnp.dot(node_features, weight, preferred_element_type=jnp.float32).astype(
        jnp.bfloat16
    )
    source_blocks = projected.reshape(blocks_dev, BLOCK, width_dev)
    products = jnp.einsum(
        "kij,kjf->kif", tile_values, source_blocks[tile_src], preferred_element_type=jnp.float32
    )
    partial_sums = jax.ops.segment_sum(products, dst_ids, num_segments=dst_segments)
    partial_sums = partial_sums.reshape(REACH, node_rows, width_dev)
    aggregated = partial_sums[0]
    for offset in range(1, REACH):
        aggregated = aggregated + passed_along(partial_sums[offset], "dom", offset)
    pre = aggregated + bias[None, :]
    output = jax.nn.silu(pre).astype(jnp.bfloat16)
    sigmoid_pre = jax.nn.sigmoid(pre)
    grad_pre = (
        out_grad.astype(jnp.float32) * sigmoid_pre * (1.0 + pre * (1.0 - sigmoid_pre))
    ).astype(jnp.bfloat16)
    panel_list = [grad_pre]
    for offset in range(1, REACH):
        panel_list.append(passed_along(grad_pre, "dom", -offset))
    stacked = jnp.stack(panel_list, axis=0).reshape(REACH * blocks_dev, BLOCK, width_dev)
    back_products = jnp.einsum(
        "kji,kjf->kif", tile_values, stacked[tile_dst], preferred_element_type=jnp.float32
    )
    upstream = jax.ops.segment_sum(back_products, src_ids, num_segments=blocks_dev)
    upstream = upstream.reshape(node_rows, width_dev).astype(jnp.bfloat16)
    weight_part = lax.dot_general(
        node_features, upstream, (((0,), (0,)), ((), ())), preferred_element_type=jnp.float32
    )
    bias_part = jnp.sum(grad_pre.astype(jnp.float32), axis=0)
    weight_grad, bias_grad = lax.psum((weight_part, bias_part), "dom")
    input_part = lax.dot_general(
        upstream, weight, (((1,), (1,)), ((), ())), preferred_element_type=jnp.float32
    )
    input_grad = lax.psum_scatter(input_part, "feat", scatter_dimension=1, tiled=True).astype(
        jnp.bfloat16
    )
    return (output, weight_grad, bias_grad, input_grad)


def solution(mesh):
    return jax.shard_map(
        shards,
        mesh=mesh,
        in_specs=(
            P("dom", None),
            P(None, "feat"),
            P("feat"),
            P("dom", None, None),
            P("dom"),
            P("dom"),
            P("dom"),
            P("dom", "feat"),
        ),
        out_specs=(P("dom", "feat"), P(None, "feat"), P("feat"), P("dom", "feat")),
        check_vma=False,
    )
```

profile of v0, /device:TPU:1, one launch (start us, length us, event | category | flops | bytes accessed | tf_op | source)
XLA Modules:
  0.0 348.8 jit_solution(1601779218866032237)
XLA Ops:
  7.2 0.0 copy-start
  7.2 0.0 reduce-scatter.2.cloned.1.call-start
  8.0 0.8 compare_select_fusion
  8.8 1.1 fusion
  10.0 1.6 gather_fusion
  11.6 0.0 copy-done
  11.6 4.0 %convolution_bitcast_fusion.1 = f32[96,128,32]{1,2,0:T(8,128)} fusion(bf16[96,128,32]{1,2,0:T(8,128)(2,1)} %gather_fusion, bf16[96,128,128]{2,1,0:T(8,128)(2,1)S(1)} %copy-done), kind=kOutput, calls=%fused_computation.5 | convolution fusion | flops 100663296 | bytes 5505024 | tf_op jit(solution)/shard_map/kij,kjf->kif/dot_general | solution.py:29
  15.6 0.8 broadcast_in_dim.24
  16.5 0.0 copy-start.2
  16.5 0.0 copy-start.4
  16.5 11.6 %scatter_fusion = f32[32,128,32]{1,2,0:T(8,128)} fusion(f32[32,128,32]{1,2,0:T(8,128)} %broadcast_in_dim.24, s32[96]{0:T(128)S(1)} %get-tuple-element.14, f32[96,128,32]{1,2,0:T(8,128)} %convolution_bitcast_fusion.1), kind=kCustom, calls=%fused_computation.2 | custom fusion | flops 393216 | bytes 4718976 | tf_op jit(solution)/shard_map/scatter-add | solution.py:32
  28.1 1.1 slice_bitcast_fusion.3
  29.3 6.2 %collective-permute-start = (f32[1024,32]{0,1:T(8,128)S(1)}, f32[1024,32]{0,1:T(8,128)S(1)}, u32[]{:S(2)}, u32[]{:S(2)}) collective-permute-start(f32[1024,32]{0,1:T(8,128)S(1)} %bitcast.66), channel_id=1, source_target_pairs={{504,0},{0,8},{8,16},{16,24},{24,32},{32,40},{40,48},{48,56},{56,6... | collective-permute-start | bytes 393224 | tf_op jit(solution)/shard_map/ppermute | solution.py:13
  35.5 3.7 %collective-permute-start.1 = (f32[1024,32]{0,1:T(8,128)S(1)}, f32[1024,32]{0,1:T(8,128)S(1)}, u32[]{:S(2)}, u32[]{:S(2)}) collective-permute-start(f32[1024,32]{0,1:T(8,128)S(1)} %bitcast.67), channel_id=1, source_target_pairs={{496,0},{504,8},{0,16},{8,24},{16,32},{24,40},{32,48},{40,56},{48,... | collective-permute-start | bytes 393224 | tf_op jit(solution)/shard_map/ppermute | solution.py:13
  39.3 3.4 collective-permute-start.2
  42.7 0.0 collective-permute-done
  42.7 6.9 %collective-permute-done.1 = f32[1024,32]{0,1:T(8,128)S(1)} collective-permute-done((f32[1024,32]{0,1:T(8,128)S(1)}, f32[1024,32]{0,1:T(8,128)S(1)}, u32[]{:S(2)}, u32[]{:S(2)}) %collective-permute-start.1) | collective-permute-done | bytes 131104 | tf_op jit(solution)/shard_map/ppermute | solution.py:13
  49.6 3.1 collective-permute-done.2
  52.7 0.0 copy-done.2
  52.7 0.0 copy-done.4
  52.7 1.3 convert_reduce_fusion
  54.1 1.9 collective-permute-start.3
  56.0 5.6 %collective-permute-start.4 = (bf16[1024,32]{0,1:T(8,128)(2,1)S(1)}, bf16[1024,32]{0,1:T(8,128)(2,1)S(1)}, u32[]{:S(2)}, u32[]{:S(2)}) collective-permute-start(bf16[1024,32]{0,1:T(8,128)(2,1)S(1)} %get-tuple-element.7), channel_id=1, source_target_pairs={{16,0},{24,8},{32,16},{40,24},{48,32},{56,40},{64,48},{72,56},{80,... | collective-permute-start | bytes 196616 | tf_op jit(solution)/shard_map/ppermute | solution.py:13
  61.6 7.1 %collective-permute-start.5 = (bf16[1024,32]{0,1:T(8,128)(2,1)S(1)}, bf16[1024,32]{0,1:T(8,128)(2,1)S(1)}, u32[]{:S(2)}, u32[]{:S(2)}) collective-permute-start(bf16[1024,32]{0,1:T(8,128)(2,1)S(1)} %get-tuple-element.7), channel_id=1, source_target_pairs={{24,0},{32,8},{40,16},{48,24},{56,32},{64,40},{72,48},{80,56},{88,... | collective-permute-start | bytes 196616 | tf_op jit(solution)/shard_map/ppermute | solution.py:13
  68.7 0.0 collective-permute-done.3
  68.7 0.0 collective-permute-done.4
  68.7 1.3 collective-permute-done.5
  70.0 0.2 copy.17
  70.3 0.8 reshape.27
  71.0 1.1 copy.18
  72.1 1.6 gather_fusion.1
  73.7 3.2 convolution_bitcast_fusion
  76.9 0.0 copy-start.3
  76.9 0.0 copy-start.1
  77.0 9.0 %scatter_fusion.1 = f32[8,128,32]{1,2,0:T(8,128)S(1)} fusion(f32[8,128,32]{1,2,0:T(8,128)S(1)} %broadcast_in_dim.28, s32[96]{0:T(128)S(1)} %get-tuple-element.18, f32[96,128,32]{1,2,0:T(8,128)} %convolution_bitcast_fusion), kind=kCustom, calls=%fused_computation.3 | custom fusion | flops 393216 | bytes 4718976 | tf_op jit(solution)/shard_map/scatter-add | solution.py:50
  86.0 0.0 copy-done.3
  86.0 1.1 fusion.4
  87.1 0.0 reduce-scatter.2.cloned.1.call-update
  87.1 1.6 multiply_convert_fusion.1
  88.7 0.0 copy-done.1
  88.7 0.2 convolution_bitcast_fusion.2
  88.8 251.6 %all-reduce = (f32[128,32]{0,1:T(8,128)}, f32[32]{0:T(128)}) all-reduce(f32[128,32]{0,1:T(8,128)S(1)} %convolution_bitcast_fusion.2, f32[32]{0:T(128)} %get-tuple-element.6), channel_id=1, replica_groups=mesh['dom'=64,'feat'=8] {'dom'}, use_global_device_ids=true, to_apply=%region_2.3 | all-reduce | flops 4128 | bytes 33024 | tf_op jit(solution)/shard_map/psum | solution.py:56
  340.5 0.0 reduce-scatter.2.cloned.1.call-done
  340.5 1.5 convert_element_type.31
  (8 shorter events, 0.1 us)
Async XLA Ops:
  7.2 4.4 %copy-start = (bf16[96,128,128]{2,1,0:T(8,128)(2,1)S(1)}, bf16[96,128,128]{2,1,0:T(8,128)(2,1)}, u32[]{:S(2)}) copy-start(bf16[96,128,128]{2,1,0:T(8,128)(2,1)} %param.11) | copy-start | bytes 9437188
  7.2 333.3 %reduce-scatter.2.cloned.1.call-start = ((), (), s32[]{:S(2)}) async-start(), calls=%async_computation.1 | async-start | bytes 589824 | tf_op jit(solution)/shard_map/reduce_scatter | solution.py:60
  16.5 36.3 %copy-start.2 = (bf16[1024,32]{0,1:T(8,128)(2,1)S(1)}, bf16[1024,32]{0,1:T(8,128)(2,1)}, u32[]{:S(2)}) copy-start(bf16[1024,32]{0,1:T(8,128)(2,1)} %param.15) | copy-start | bytes 196612
  16.5 36.3 %copy-start.4 = (f32[32]{0:T(128)S(1)}, f32[32]{0:T(128)}, u32[]{:S(2)}) copy-start(f32[32]{0:T(128)} %param.10) | copy-start | bytes 388
  29.3 13.4 %collective-permute-start = (f32[1024,32]{0,1:T(8,128)S(1)}, f32[1024,32]{0,1:T(8,128)S(1)}, u32[]{:S(2)}, u32[]{:S(2)}) collective-permute-start(f32[1024,32]{0,1:T(8,128)S(1)} %bitcast.66), channel_id=1, source_target_pairs={{504,0},{0,8},{8,16},{16,24},{24,32},{32,40},{40,48},{48,56},{56,6... | collective-permute-start | bytes 393224 | tf_op jit(solution)/shard_map/ppermute | solution.py:13
  35.5 14.1 %collective-permute-start.1 = (f32[1024,32]{0,1:T(8,128)S(1)}, f32[1024,32]{0,1:T(8,128)S(1)}, u32[]{:S(2)}, u32[]{:S(2)}) collective-permute-start(f32[1024,32]{0,1:T(8,128)S(1)} %bitcast.67), channel_id=1, source_target_pairs={{496,0},{504,8},{0,16},{8,24},{16,32},{24,40},{32,48},{40,56},{48,... | collective-permute-start | bytes 393224 | tf_op jit(solution)/shard_map/ppermute | solution.py:13
  39.3 13.5 %collective-permute-start.2 = (f32[1024,32]{0,1:T(8,128)S(1)}, f32[1024,32]{0,1:T(8,128)S(1)}, u32[]{:S(2)}, u32[]{:S(2)}) collective-permute-start(f32[1024,32]{0,1:T(8,128)S(1)} %bitcast.68), channel_id=1, source_target_pairs={{488,0},{496,8},{504,16},{0,24},{8,32},{16,40},{24,48},{32,56},{40... | collective-permute-start | bytes 393224 | tf_op jit(solution)/shard_map/ppermute | solution.py:13
  54.1 14.6 %collective-permute-start.3 = (bf16[1024,32]{0,1:T(8,128)(2,1)S(1)}, bf16[1024,32]{0,1:T(8,128)(2,1)S(1)}, u32[]{:S(2)}, u32[]{:S(2)}) collective-permute-start(bf16[1024,32]{0,1:T(8,128)(2,1)S(1)} %get-tuple-element.7), channel_id=1, source_target_pairs={{8,0},{16,8},{24,16},{32,24},{40,32},{48,40},{56,48},{64,56},{72,6... | collective-permute-start | bytes 196616 | tf_op jit(solution)/shard_map/ppermute | solution.py:13
  56.0 12.7 %collective-permute-start.4 = (bf16[1024,32]{0,1:T(8,128)(2,1)S(1)}, bf16[1024,32]{0,1:T(8,128)(2,1)S(1)}, u32[]{:S(2)}, u32[]{:S(2)}) collective-permute-start(bf16[1024,32]{0,1:T(8,128)(2,1)S(1)} %get-tuple-element.7), channel_id=1, source_target_pairs={{16,0},{24,8},{32,16},{40,24},{48,32},{56,40},{64,48},{72,56},{80,... | collective-permute-start | bytes 196616 | tf_op jit(solution)/shard_map/ppermute | solution.py:13
  61.6 8.4 %collective-permute-start.5 = (bf16[1024,32]{0,1:T(8,128)(2,1)S(1)}, bf16[1024,32]{0,1:T(8,128)(2,1)S(1)}, u32[]{:S(2)}, u32[]{:S(2)}) collective-permute-start(bf16[1024,32]{0,1:T(8,128)(2,1)S(1)} %get-tuple-element.7), channel_id=1, source_target_pairs={{24,0},{32,8},{40,16},{48,24},{56,32},{64,40},{72,48},{80,56},{88,... | collective-permute-start | bytes 196616 | tf_op jit(solution)/shard_map/ppermute | solution.py:13
  76.9 9.1 %copy-start.3 = (bf16[128,32]{0,1:T(8,128)(2,1)S(1)}, bf16[128,32]{0,1:T(8,128)(2,1)}, u32[]{:S(2)}) copy-start(bf16[128,32]{0,1:T(8,128)(2,1)} %param.9) | copy-start | bytes 24580
  76.9 11.7 %copy-start.1 = (bf16[1024,128]{1,0:T(8,128)(2,1)S(1)}, bf16[1024,128]{1,0:T(8,128)(2,1)}, u32[]{:S(2)}) copy-start(bf16[1024,128]{1,0:T(8,128)(2,1)} %param.8) | copy-start | bytes 786436
Sparse Core Ops, SparseCore 0:
  87.2 39.1 reduce-scatter.1
where the time goes:
time: 354 us; the launch traced here: 349 us
  blocking collectives  252 us (71%)
  starting transfers between devices  28 us (8%)
  other arithmetic  25.9 us (7%)
  between operations  15 us (4%)
  waiting for transfers between devices  11.3 us (3%)
  matrix products  9.61 us (3%)
  local copies, waits for them, and re-layouts  7.3 us (2%)
    psum x1, blocking collectives, shards(): weight_grad, bias_grad = lax.psum((weight_part, bias_part), 'dom')  252 us
    ppermute x6, starting transfers between devices, passed_along(): return lax.ppermute(block, axis, route)  27.9 us
    scatter-add x1, other arithmetic, shards(): jax.ops.segment_sum(products, dst_ids, num_segments=dst_segments)  11.6 us
    ppermute x6, waiting for transfers between devices, passed_along(): return lax.ppermute(block, axis, route)  11.3 us
    scatter-add x1, other arithmetic, shards(): jax.ops.segment_sum(back_products, src_ids, num_segments=blocks_dev)  9.05 us
  transfers between devices with their start and end apart: 7, of which 3 were waited for; matrix products, arithmetic and copies ran while one was open for 1% of the time, Pallas kernels for 0%

commit v1 on v0

v1 whole, which is shorter than its diff:
```python
import functools

import jax
import jax.numpy as jnp
from jax import lax
from jax.experimental import pallas as pl
from jax.experimental.pallas import tpu as pltpu
from jax.sharding import PartitionSpec as P

REACH = 4
NB = 8
BLOCK = 128
NFEAT = 8
FW = 16
PER_OFFSET = 24
HID_DEV = 32
GROUP = 4
MESH = pl.DeviceIdType.MESH
F32 = jnp.float32
BF16 = jnp.bfloat16
ORDER = (3, 2, 1, 0)


def kernel(
    n_dom,
    nf_hbm, wt, bias, tiles_hbm, src, dst, cnt, og_hbm,
    out, wg, bg, ig,
    nf, og, tiles, nft, table, psend, precv, agg, hsend, hrecv, hall0, hall1, hall2, hall3,
    rsend, rrecv, zbuf, wfin,
    load_sem, tile_sem, p_sem, a_sem, h_sem, b_sem, r_sem, z_sem, w_sem,
):
    n_z = n_dom // GROUP
    hall = (hall0, hall1, hall2, hall3)
    dom = lax.axis_index("dom")
    feat = lax.axis_index("feat")
    z = dom // GROUP
    lane = lax.rem(dom, GROUP)

    def dom_at(step):
        return lax.rem(dom + (step % n_dom), n_dom)

    def feat_at(step):
        return lax.rem(feat + step, NFEAT)

    def group_at(step):
        return lax.rem(lane + step, GROUP)

    def z_at(step):
        return lax.rem(z + step, n_z)

    barrier = pltpu.get_barrier_semaphore()

    def greet(device):
        pl.semaphore_signal(barrier, inc=1, device_id=device, device_id_type=MESH)

    loads = [
        pltpu.make_async_copy(nf_hbm, nf, load_sem.at[0]),
        pltpu.make_async_copy(og_hbm, og, load_sem.at[1]),
    ]
    tile_loads = {
        o: pltpu.make_async_copy(tiles_hbm.at[:, o], tiles.at[o], tile_sem.at[o])
        for o in range(REACH)
    }
    loads[0].start()
    for o in ORDER:
        tile_loads[o].start()
    loads[1].start()

    for step in range(1, REACH):
        greet((dom_at(step), feat))
        greet((dom_at(-step), feat))
    for step in range(1, NFEAT):
        greet((dom, feat_at(step)))
    for step in range(1, n_z):
        greet((z_at(step) * GROUP + lane, feat))
    greetings = 2 * (REACH - 1) + NFEAT - 1 + n_z - 1

    def send(src_ref, dst_ref, sems, s, r, device):
        copy = pltpu.make_async_remote_copy(
            src_ref=src_ref,
            dst_ref=dst_ref,
            send_sem=sems.at[0, s],
            recv_sem=sems.at[1, r],
            device_id=device,
            device_id_type=MESH,
        )
        copy.start()
        return copy

    def arrival(ref, sems, r):
        pltpu.make_async_copy(ref, ref, sems.at[1, r]).wait()

    one = jnp.ones((FW, BLOCK), BF16)
    zero = jnp.zeros((FW, BLOCK), BF16)
    for g in range(NB + 1):
        for row in range(NB):
            table[g, row * FW : (row + 1) * FW, :] = one if row == g else zero

    loads[0].wait()
    rows = lax.broadcasted_iota(jnp.int32, (FW, BLOCK), 0)
    columns = lax.broadcasted_iota(jnp.int32, (FW, BLOCK), 1)
    pick = jnp.where(columns == rows + feat * FW, 1.0, 0.0).astype(BF16)
    picked = lax.dot_general(
        pick, nf[...], (((1,), (1,)), ((), ())), preferred_element_type=F32
    ).astype(BF16)
    for b in range(NB):
        nft[b] = picked[:, b * BLOCK : (b + 1) * BLOCK]

    used = cnt[0]

    def placed(block, position, k):
        position = jnp.where(k < used, position, NB)
        return jnp.concatenate([block] * NB, axis=0) * table[position]

    def forward(o):
        left = []
        right = []
        for j in range(PER_OFFSET):
            k = j * REACH + o
            left.append(placed(nft[src[k]], dst[k] & (NB - 1), k))
            right.append(tiles[o, j])
        return lax.dot_general(
            jnp.concatenate(left, axis=1),
            jnp.concatenate(right, axis=1),
            (((1,), (1,)), ((), ())),
            preferred_element_type=F32,
        )

    sends = []
    own = None
    for o in ORDER:
        tile_loads[o].wait()
        part = forward(o)
        if o == 0:
            own = part
        else:
            psend[o - 1] = part.astype(BF16)
            if o == ORDER[0]:
                pl.semaphore_wait(barrier, greetings)
            sends.append(
                send(psend.at[o - 1], precv.at[o - 1], p_sem, o - 1, o - 1, (dom_at(o), feat))
            )
    for o in ORDER:
        if o:
            arrival(precv.at[o - 1], p_sem, o - 1)
            own = own + precv[o - 1].astype(F32)
    agg[feat] = own.astype(BF16)
    for step in range(1, NFEAT):
        sends.append(
            send(agg.at[feat], agg.at[feat], a_sem, step, feat, (dom, feat_at(step)))
        )
    loads[1].wait()
    bias_square = jnp.broadcast_to(bias[...], (HID_DEV, HID_DEV))
    on_diagonal = lax.broadcasted_iota(jnp.int32, (HID_DEV, HID_DEV), 0) == (
        lax.broadcasted_iota(jnp.int32, (HID_DEV, HID_DEV), 1)
    )
    bias_column = jnp.sum(jnp.where(on_diagonal, bias_square, 0.0), axis=1, keepdims=True)
    for step in range(1, NFEAT):
        arrival(agg.at[feat_at(step)], a_sem, feat_at(step))
    aggregated = jnp.concatenate(
        [
            jnp.concatenate([agg[i, g * FW : (g + 1) * FW, :] for i in range(NFEAT)], axis=0)
            for g in range(NB)
        ],
        axis=1,
    )
    pre = (
        jnp.dot(wt[...], aggregated, preferred_element_type=F32) + bias_column
    )
    sigmoid_pre = jax.nn.sigmoid(pre)
    grad_pre = (
        og[...].astype(F32) * sigmoid_pre * (1.0 + pre * (1.0 - sigmoid_pre))
    ).astype(BF16)
    back = lax.dot_general(
        wt[...], grad_pre, (((0,), (0,)), ((), ())), preferred_element_type=F32
    ).astype(BF16)
    for i in range(NFEAT):
        for g in range(NB):
            hsend[i, g * FW : (g + 1) * FW, :] = back[
                i * FW : (i + 1) * FW, g * BLOCK : (g + 1) * BLOCK
            ]
    for step in range(1, NFEAT):
        sends.append(
            send(
                hsend.at[feat_at(step)], hrecv.at[feat], h_sem, step, feat, (dom, feat_at(step))
            )
        )
    hrecv[feat] = hsend[feat]
    out[...] = (pre * sigmoid_pre).astype(BF16)

    weight_part = lax.dot_general(
        grad_pre, aggregated, (((1,), (1,)), ((), ())), preferred_element_type=F32
    )
    bias_part = lax.dot_general(
        jnp.ones((8, NB * BLOCK), BF16),
        jnp.concatenate([grad_pre] * 4, axis=0),
        (((1,), (1,)), ((), ())),
        preferred_element_type=F32,
    )
    for c in range(GROUP):
        rsend[c, 0:8, :] = weight_part[c * 8 : (c + 1) * 8, :]
        rsend[c, 8:16, :] = bias_part
    for step in range(1, GROUP):
        sends.append(
            send(
                rsend.at[group_at(step)], rrecv.at[lane], r_sem, step, lane,
                (z * GROUP + group_at(step), feat),
            )
        )
    rrecv[lane] = rsend[lane]

    for step in range(1, NFEAT):
        arrival(hrecv.at[feat_at(step)], h_sem, feat_at(step))
    mixed = hrecv[0].astype(F32)
    for i in range(1, NFEAT):
        mixed = mixed + hrecv[i].astype(F32)
    mixed = mixed.astype(BF16)
    for g in range(NB):
        hall0[g] = mixed[g * FW : (g + 1) * FW, :]
    for o in ORDER[:-1]:
        sends.append(
            send(hall0, hall[o], b_sem, o, o, (dom_at(-o), feat))
        )

    for step in range(1, GROUP):
        arrival(rrecv.at[group_at(step)], r_sem, group_at(step))
    zbuf[z] = jnp.sum(rrecv[...], axis=0)
    for step in range(1, n_z):
        sends.append(
            send(zbuf.at[z], zbuf.at[z], z_sem, step, z, (z_at(step) * GROUP + lane, feat))
        )

    def backward(o):
        left = []
        for j in range(PER_OFFSET):
            k = j * REACH + o
            left.append(placed(hall[o][dst[k] & (NB - 1)], src[k], k))
        return jnp.dot(
            jnp.concatenate(left, axis=1),
            tiles[o].reshape(PER_OFFSET * BLOCK, BLOCK),
            preferred_element_type=F32,
        )

    total = backward(0)
    for o in (1, 2):
        arrival(hall[o], b_sem, o)
        total = total + backward(o)

    for step in range(1, n_z):
        arrival(zbuf.at[z_at(step)], z_sem, z_at(step))
    wfin[lane] = jnp.sum(zbuf[...], axis=0)
    for step in range(1, GROUP):
        sends.append(
            send(
                wfin.at[lane], wfin.at[lane], w_sem, step, lane,
                (z * GROUP + group_at(step), feat),
            )
        )
    arrival(hall3, b_sem, 3)
    total = (total + backward(3)).astype(BF16)
    for g in range(NB):
        ig[:, g * BLOCK : (g + 1) * BLOCK] = total[g * FW : (g + 1) * FW, :]
    for step in range(1, GROUP):
        arrival(wfin.at[group_at(step)], w_sem, group_at(step))
    for c in range(GROUP):
        wg[c * 8 : (c + 1) * 8, :] = wfin[c, 0:8, :]
    bg[...] = wfin[0, 8:9, 0:HID_DEV]
    for copy in sends:
        copy.wait_send()


def shards(node_features, weight, bias, tile_values, tile_src, tile_dst, tile_counts, out_grad):
    n_dom = lax.axis_size("dom")
    n_z = n_dom // GROUP
    nodes = NB * BLOCK
    vmem = pl.BlockSpec(memory_space=pltpu.VMEM)
    smem = pl.BlockSpec(memory_space=pltpu.SMEM)
    hbm = pl.BlockSpec(memory_space=pltpu.HBM)
    dma = pltpu.SemaphoreType.DMA
    out, wg, bg, ig = pl.pallas_call(
        functools.partial(kernel, n_dom),
        out_shape=(
            jax.ShapeDtypeStruct((HID_DEV, nodes), BF16),
            jax.ShapeDtypeStruct((HID_DEV, BLOCK), F32),
            jax.ShapeDtypeStruct((1, HID_DEV), F32),
            jax.ShapeDtypeStruct((FW, nodes), BF16),
        ),
        in_specs=[hbm, vmem, vmem, hbm, smem, smem, smem, hbm],
        out_specs=(vmem, vmem, vmem, vmem),
        scratch_shapes=[
            pltpu.VMEM((nodes, BLOCK), BF16),
            pltpu.VMEM((HID_DEV, nodes), BF16),
            pltpu.VMEM((REACH, PER_OFFSET, BLOCK, BLOCK), BF16),
            pltpu.VMEM((NB, FW, BLOCK), BF16),
            pltpu.VMEM((NB + 1, BLOCK, BLOCK), BF16),
            pltpu.VMEM((REACH - 1, BLOCK, BLOCK), BF16),
            pltpu.VMEM((REACH - 1, BLOCK, BLOCK), BF16),
            pltpu.VMEM((NFEAT, BLOCK, BLOCK), BF16),
            pltpu.VMEM((NFEAT, BLOCK, BLOCK), BF16),
            pltpu.VMEM((NFEAT, BLOCK, BLOCK), BF16),
            pltpu.VMEM((NB, FW, BLOCK), BF16),
            pltpu.VMEM((NB, FW, BLOCK), BF16),
            pltpu.VMEM((NB, FW, BLOCK), BF16),
            pltpu.VMEM((NB, FW, BLOCK), BF16),
            pltpu.VMEM((GROUP, 16, BLOCK), F32),
            pltpu.VMEM((GROUP, 16, BLOCK), F32),
            pltpu.VMEM((n_z, 16, BLOCK), F32),
            pltpu.VMEM((GROUP, 16, BLOCK), F32),
            dma((2,)),
            dma((REACH,)),
            dma((2, REACH - 1)),
            dma((2, NFEAT)),
            dma((2, NFEAT)),
            dma((2, REACH)),
            dma((2, GROUP)),
            dma((2, n_z)),
            dma((2, GROUP)),
        ],
        compiler_params=pltpu.CompilerParams(
            collective_id=0, has_side_effects=True
        ),
        name="graph_layer",
    )(
        node_features,
        weight.T,
        bias.reshape(1, HID_DEV),
        tile_values.reshape(PER_OFFSET, REACH, BLOCK, BLOCK),
        tile_src,
        tile_dst,
        tile_counts,
        out_grad.T,
    )
    return out.T, wg.T, bg.reshape(HID_DEV), ig.T


def solution(mesh):
    return jax.shard_map(
        shards,
        mesh=mesh,
        in_specs=(
            P("dom", None),
            P(None, "feat"),
            P("feat"),
            P("dom", None, None),
            P("dom"),
            P("dom"),
            P("dom"),
            P("dom", "feat"),
        ),
        out_specs=(P("dom", "feat"), P(None, "feat"), P("feat"), P("dom", "feat")),
        check_vma=False,
    )
```

time: 354 us -> 57.7 us (0.16); the launches traced: 349 us -> 57.4 us
  blocking collectives: 252 us -> 0 us
  Pallas kernels: 0 us -> 50.8 us
  starting transfers between devices: 28 us -> 0 us
  other arithmetic: 25.9 us -> 0 us
  between operations: 15 us -> 1.29 us
  waiting for transfers between devices: 11.3 us -> 0 us
  matrix products: 9.61 us -> 0 us
    psum x1 -> x0, blocking collectives: 252 us -> none  [shards(): weight_grad, bias_grad = lax.psum((weight_part, bias_part), 'dom')]
    pallas_call x0 -> x1, Pallas kernels: none -> 50.8 us  [shards(): pl.pallas_call(functools.partial(kernel, n_dom), out_shape=(jax.ShapeDtyp...]
    ppermute x6 -> x0, starting transfers between devices: 27.9 us -> none  [passed_along(): return lax.ppermute(block, axis, route)]
    scatter-add x2 -> x0, other arithmetic: 20.7 us -> none  [the longest x1 11.6 us: shards(): jax.ops.segment_sum(products, dst_ids, num_segments=dst_segments)]
    ppermute x6 -> x0, waiting for transfers between devices: 11.3 us -> none  [passed_along(): return lax.ppermute(block, axis, route)]
    dot_general x5 -> x0, matrix products: 9.61 us -> none  [the longest x1 4.05 us: shards(): jnp.einsum('kij,kjf->kif', tile_values, source_blocks[tile_src], preferre...]
    unnamed x11 -> x4, local copies, waits for them, and re-layouts: 1.16 us -> 5.28 us
  transfers between devices with their start and end apart: 7 -> 0, of which waited for: 3 -> 0; matrix products, arithmetic and copies ran while one was open for 1% -> 0% of each run, Pallas kernels for 0% -> 0%
where the time goes in v1:
time: 57.7 us; the launch traced here: 57.4 us
  Pallas kernels  50.8 us (88%)
  local copies, waits for them, and re-layouts  5.28 us (9%)
  between operations  1.29 us (2%)
    pallas_call x1, Pallas kernels, shards(): pl.pallas_call(functools.partial(kernel, n_dom), out_shape=(jax.ShapeDtyp...  50.8 us
    unnamed x4, local copies, waits for them, and re-layouts  5.28 us

profile of v1, /device:TPU:1, one launch (start us, length us, event | category | flops | bytes accessed | tf_op | source)
XLA Modules:
  0.0 57.4 jit_solution(13754583855454650654)
XLA Ops:
  1.3 50.8 %graph_layer.1 = (bf16[32,1024]{1,0:T(8,128)(2,1)}, f32[32,128]{1,0:T(8,128)}, f32[1,32]{1,0:T(1,128)}, bf16[16,1024]{1,0:T(8,128)(2,1)}) custom-call(bf16[1024,128]{1,0:T(8,128)(2,1)} %nf_hbm.1, bf16[32,128]{1,0:T(8,128)(2,1)} %bitcast.13, f32[1,32]{1,0:T(1,128)} %bitcast.14, bf16[24,4,128,128]{3,2,1,0:T(8,128)(2,1)} %bitcast.8, s32[96]{0:T(128)} %src.1, ...), custom_call_target="tpu_custom_call" | custom-call | tf_op jit(solution)/shard_map/graph_layer/pallas_call | solution.py:280
  52.1 1.5 %copy.17 = bf16[1024,32]{0,1:T(8,128)(2,1)} copy(bf16[1024,32]{0,1:T(8,128)(2,1)} %bitcast.10) | data formatting | bytes 131072
  53.6 1.3 %copy.18 = f32[128,32]{0,1:T(8,128)} copy(f32[128,32]{0,1:T(8,128)} %bitcast.12) | data formatting | bytes 32768
  54.9 1.1 %copy.19 = f32[32]{0:T(128)} copy(f32[32]{0:T(128)} %bitcast.15) | data formatting | bytes 256
  56.0 1.4 %copy.20 = bf16[1024,16]{0,1:T(8,128)(2,1)} copy(bf16[1024,16]{0,1:T(8,128)(2,1)} %bitcast.11) | data formatting | bytes 65536

commit v2 on v1

v2 whole, which is shorter than its diff:
```python
import functools

import jax
import jax.numpy as jnp
from jax import lax
from jax.experimental import pallas as pl
from jax.experimental.pallas import tpu as pltpu
from jax.sharding import PartitionSpec as P

REACH = 4
NB = 8
BLOCK = 128
NFEAT = 8
FW = 16
PER_OFFSET = 24
HID_DEV = 32
GROUP = 4
MESH = pl.DeviceIdType.MESH
F32 = jnp.float32
BF16 = jnp.bfloat16
ORDER = (3, 2, 1, 0)


def kernel(
    n_dom,
    nf_hbm, wt_hbm, bias_hbm, tiles_hbm, src_hbm, dst_hbm, cnt, og_hbm,
    out, wg, bg, ig,
    nf, og, wt, bias, src, dst, tiles, nft, table, psend, precv, agg, hsend, hrecv,
    hall0, hall1, hall2, hall3,
    rsend, rrecv, rbias, ysend, yrecv, ybias, zbuf, zbias, wfin,
    load_sem, tile_sem, p_sem, a_sem, h_sem, b_sem, r_sem, y_sem, z_sem, zb_sem, w_sem,
    relay_sem,
):
    n_z = n_dom // GROUP
    hall = (hall0, hall1, hall2, hall3)
    dom = lax.axis_index("dom")
    feat = lax.axis_index("feat")
    z = dom // GROUP
    lane = lax.rem(dom, GROUP)
    core = lax.rem(dom, 2)
    partner = (dom + 1 - 2 * core, feat)
    across = (z * GROUP + lax.rem(lane + 2, GROUP), feat)

    def dom_at(step):
        return lax.rem(dom + (step % n_dom), n_dom)

    def feat_at(step):
        return lax.rem(feat + step, NFEAT)

    def z_at(step):
        return lax.rem(z + step, n_z)

    def z_peer(step):
        return (z_at(step) * GROUP + lane, feat)

    def around(*distances):
        return sorted({d % n_z for r in distances for d in (r, -r)} - {0})

    barrier = pltpu.get_barrier_semaphore()

    def signal(sem, device):
        pl.semaphore_signal(sem, inc=1, device_id=device, device_id_type=MESH)

    near = [(dom_at(step), feat) for step in range(1, REACH)]
    near += [(dom_at(-step), feat) for step in range(1, REACH)]
    near += [(dom, feat_at(step)) for step in range(1, NFEAT)]
    near += [z_peer(step) for step in around(1, 2)]
    for device in near:
        signal(barrier, device)

    pairs = [
        (src_hbm, src), (dst_hbm, dst), (nf_hbm, nf),
        (wt_hbm, wt), (bias_hbm, bias), (og_hbm, og),
    ]
    loads = [pltpu.make_async_copy(a, b, load_sem.at[i]) for i, (a, b) in enumerate(pairs)]
    tile_loads = [
        pltpu.make_async_copy(tiles_hbm.at[:, o], tiles.at[o], tile_sem.at[o])
        for o in range(REACH)
    ]
    for load in loads[:3]:
        load.start()
    for o in ORDER:
        tile_loads[o].start()
    for load in loads[3:]:
        load.start()

    sends = []

    def send(src_ref, dst_ref, sems, s, r, device):
        copy = pltpu.make_async_remote_copy(
            src_ref=src_ref,
            dst_ref=dst_ref,
            send_sem=sems.at[0, s],
            recv_sem=sems.at[1, r],
            device_id=device,
            device_id_type=MESH,
        )
        copy.start()
        sends.append(copy)

    def arrival(ref, sems, r):
        pltpu.make_async_copy(ref, ref, sems.at[1, r]).wait()

    one = jnp.ones((FW, BLOCK), BF16)
    zero = jnp.zeros((FW, BLOCK), BF16)
    for g in range(NB + 1):
        for row in range(NB):
            table[g, row * FW : (row + 1) * FW, :] = one if row == g else zero

    rows = lax.broadcasted_iota(jnp.int32, (FW, BLOCK), 0)
    columns = lax.broadcasted_iota(jnp.int32, (FW, BLOCK), 1)
    pick = jnp.where(columns == rows + feat * FW, 1.0, 0.0).astype(BF16)
    for load in loads[:3]:
        load.wait()
    picked = lax.dot_general(
        pick, nf[...], (((1,), (1,)), ((), ())), preferred_element_type=F32
    ).astype(BF16)
    for b in range(NB):
        nft[b] = picked[:, b * BLOCK : (b + 1) * BLOCK]

    used = cnt[0]

    def placed(block, position, k):
        position = jnp.where(k < used, position, NB)
        return jnp.concatenate([block] * NB, axis=0) * table[position]

    def forward(o):
        left = []
        right = []
        for j in range(PER_OFFSET):
            k = j * REACH + o
            left.append(placed(nft[src[k]], dst[k] & (NB - 1), k))
            right.append(tiles[o, j])
        return lax.dot_general(
            jnp.concatenate(left, axis=1),
            jnp.concatenate(right, axis=1),
            (((1,), (1,)), ((), ())),
            preferred_element_type=F32,
        )

    for o in ORDER[:-1]:
        tile_loads[o].wait()
        psend[o - 1] = forward(o).astype(BF16)
    tile_loads[0].wait()
    own = forward(0)
    for load in loads[3:]:
        load.wait()
    pl.semaphore_wait(barrier, len(near))
    for o in ORDER[:-1]:
        send(psend.at[o - 1], precv.at[o - 1], p_sem, o - 1, o - 1, (dom_at(o), feat))
    for step in around(2):
        signal(relay_sem.at[0], z_peer(step))
    bias_square = jnp.broadcast_to(bias[...], (HID_DEV, HID_DEV))
    on_diagonal = lax.broadcasted_iota(jnp.int32, (HID_DEV, HID_DEV), 0) == (
        lax.broadcasted_iota(jnp.int32, (HID_DEV, HID_DEV), 1)
    )
    bias_column = jnp.sum(jnp.where(on_diagonal, bias_square, 0.0), axis=1, keepdims=True)
    for o in ORDER[:-1]:
        arrival(precv.at[o - 1], p_sem, o - 1)
        own = own + precv[o - 1].astype(F32)
    agg[feat] = own.astype(BF16)
    for step in range(1, NFEAT):
        send(agg.at[feat], agg.at[feat], a_sem, step, feat, (dom, feat_at(step)))
    if around(2):
        pl.semaphore_wait(relay_sem.at[0], len(around(2)))
    for step in around(4):
        signal(relay_sem.at[1], z_peer(step))
    for step in range(1, NFEAT):
        arrival(agg.at[feat_at(step)], a_sem, feat_at(step))
    aggregated = jnp.concatenate(
        [
            jnp.concatenate([agg[i, g * FW : (g + 1) * FW, :] for i in range(NFEAT)], axis=0)
            for g in range(NB)
        ],
        axis=1,
    )
    pre = jnp.dot(wt[...], aggregated, preferred_element_type=F32) + bias_column
    sigmoid_pre = jax.nn.sigmoid(pre)
    grad_pre = (
        og[...].astype(F32) * sigmoid_pre * (1.0 + pre * (1.0 - sigmoid_pre))
    ).astype(BF16)

    weight_part = lax.dot_general(
        grad_pre, aggregated, (((1,), (1,)), ((), ())), preferred_element_type=F32
    )
    bias_part = lax.dot_general(
        jnp.ones((8, NB * BLOCK), BF16),
        jnp.concatenate([grad_pre] * 4, axis=0),
        (((1,), (1,)), ((), ())),
        preferred_element_type=F32,
    )
    rsend[0] = weight_part[0:16, :]
    rsend[1] = weight_part[16:32, :]
    rbias[0] = bias_part[0:1, :]
    send(rsend.at[1 - core], rrecv, r_sem, 0, 0, partner)
    send(rbias.at[0], rbias.at[1], r_sem, 1, 1, partner)

    back = lax.dot_general(
        wt[...], grad_pre, (((0,), (0,)), ((), ())), preferred_element_type=F32
    ).astype(BF16)
    for i in range(NFEAT):
        for g in range(NB):
            hsend[i, g * FW : (g + 1) * FW, :] = back[
                i * FW : (i + 1) * FW, g * BLOCK : (g + 1) * BLOCK
            ]
    for step in range(1, NFEAT):
        send(hsend.at[feat_at(step)], hrecv.at[feat], h_sem, step, feat, (dom, feat_at(step)))
    hrecv[feat] = hsend[feat]

    arrival(rrecv, r_sem, 0)
    arrival(rbias.at[1], r_sem, 1)
    ysend[...] = rsend[core] + rrecv[...]
    ybias[0] = rbias[0] + rbias[1]
    send(ysend, yrecv, y_sem, 0, 0, across)
    send(ybias.at[0], ybias.at[1], y_sem, 1, 1, across)
    out[...] = (pre * sigmoid_pre).astype(BF16)
    if around(4):
        pl.semaphore_wait(relay_sem.at[1], len(around(4)))
    arrival(yrecv, y_sem, 0)
    arrival(ybias.at[1], y_sem, 1)
    zbuf[z] = (ysend[...] + yrecv[...]).astype(BF16)
    zbias[z] = ybias[0] + ybias[1]
    for step in range(1, n_z):
        send(zbuf.at[z], zbuf.at[z], z_sem, step, z, z_peer(step))
        send(zbias.at[z], zbias.at[z], zb_sem, step, z, z_peer(step))

    for step in range(1, NFEAT):
        arrival(hrecv.at[feat_at(step)], h_sem, feat_at(step))
    mixed = hrecv[0].astype(F32)
    for i in range(1, NFEAT):
        mixed = mixed + hrecv[i].astype(F32)
    mixed = mixed.astype(BF16)
    for g in range(NB):
        hall0[g] = mixed[g * FW : (g + 1) * FW, :]
    for o in ORDER[:-1]:
        send(hall0, hall[o], b_sem, o, o, (dom_at(-o), feat))

    def backward(o):
        left = []
        for j in range(PER_OFFSET):
            k = j * REACH + o
            left.append(placed(hall[o][dst[k] & (NB - 1)], src[k], k))
        return jnp.dot(
            jnp.concatenate(left, axis=1),
            tiles[o].reshape(PER_OFFSET * BLOCK, BLOCK),
            preferred_element_type=F32,
        )

    total = backward(0)
    for o in (1, 2, 3):
        arrival(hall[o], b_sem, o)
        total = total + backward(o)
    total = total.astype(BF16)
    for g in range(NB):
        ig[:, g * BLOCK : (g + 1) * BLOCK] = total[g * FW : (g + 1) * FW, :]

    for step in range(1, n_z):
        arrival(zbuf.at[z_at(step)], z_sem, z_at(step))
    wfin[core] = jnp.sum(zbuf[...].astype(F32), axis=0)
    send(wfin.at[core], wfin.at[core], w_sem, 0, core, partner)
    for step in range(1, n_z):
        arrival(zbias.at[z_at(step)], zb_sem, z_at(step))
    bg[...] = jnp.sum(zbias[...], axis=0)[:, 0:HID_DEV]
    arrival(wfin.at[1 - core], w_sem, 1 - core)
    wg[0:16, :] = wfin[0]
    wg[16:32, :] = wfin[1]
    for copy in sends:
        copy.wait_send()


def finish(*refs):
    values, outs, sem = refs[:4], refs[4:8], refs[8]
    copies = [pltpu.make_async_copy(a, b, sem.at[i]) for i, (a, b) in enumerate(zip(values, outs))]
    for copy in copies:
        copy.start()
    for copy in copies:
        copy.wait()


def shards(node_features, weight, bias, tile_values, tile_src, tile_dst, tile_counts, out_grad):
    n_dom = lax.axis_size("dom")
    n_z = n_dom // GROUP
    nodes = NB * BLOCK
    vmem = pl.BlockSpec(memory_space=pltpu.VMEM)
    hbm = pl.BlockSpec(memory_space=pltpu.HBM)
    anywhere = pl.BlockSpec(memory_space=pl.ANY)
    dma = pltpu.SemaphoreType.DMA
    block = pltpu.VMEM((NB, FW, BLOCK), BF16)
    square = pltpu.VMEM((NFEAT, BLOCK, BLOCK), BF16)
    limit = 24 * 1024 * 1024
    shapes = (
        jax.ShapeDtypeStruct((HID_DEV, nodes), BF16),
        jax.ShapeDtypeStruct((HID_DEV, BLOCK), F32),
        jax.ShapeDtypeStruct((1, HID_DEV), F32),
        jax.ShapeDtypeStruct((FW, nodes), BF16),
    )
    results = pl.pallas_call(
        functools.partial(kernel, n_dom),
        out_shape=shapes,
        in_specs=[hbm] * 6 + [pl.BlockSpec(memory_space=pltpu.SMEM), hbm],
        out_specs=(vmem,) * 4,
        scratch_shapes=[
            pltpu.VMEM((nodes, BLOCK), BF16),
            pltpu.VMEM((HID_DEV, nodes), BF16),
            pltpu.VMEM((HID_DEV, BLOCK), BF16),
            pltpu.VMEM((1, HID_DEV), F32),
            pltpu.SMEM((PER_OFFSET * REACH,), jnp.int32),
            pltpu.SMEM((PER_OFFSET * REACH,), jnp.int32),
            pltpu.VMEM((REACH, PER_OFFSET, BLOCK, BLOCK), BF16),
            block,
            pltpu.VMEM((NB + 1, BLOCK, BLOCK), BF16),
            pltpu.VMEM((REACH - 1, BLOCK, BLOCK), BF16),
            pltpu.VMEM((REACH - 1, BLOCK, BLOCK), BF16),
            square,
            square,
            square,
            block,
            block,
            block,
            block,
            pltpu.VMEM((2, 16, BLOCK), F32),
            pltpu.VMEM((16, BLOCK), F32),
            pltpu.VMEM((2, 1, BLOCK), F32),
            pltpu.VMEM((16, BLOCK), F32),
            pltpu.VMEM((16, BLOCK), F32),
            pltpu.VMEM((2, 1, BLOCK), F32),
            pltpu.VMEM((n_z, 16, BLOCK), BF16),
            pltpu.VMEM((n_z, 1, BLOCK), F32),
            pltpu.VMEM((2, 16, BLOCK), F32),
            dma((6,)),
            dma((REACH,)),
            dma((2, REACH - 1)),
            dma((2, NFEAT)),
            dma((2, NFEAT)),
            dma((2, REACH)),
            dma((2, 2)),
            dma((2, 2)),
            dma((2, n_z)),
            dma((2, n_z)),
            dma((2, 2)),
            pltpu.SemaphoreType.REGULAR((2,)),
        ],
        compiler_params=pltpu.CompilerParams(
            collective_id=0, has_side_effects=True, vmem_limit_bytes=limit
        ),
        name="graph_layer",
    )(
        *(
            x if x is tile_counts else pltpu.with_memory_space_constraint(x, pltpu.HBM)
            for x in (
                node_features,
                weight.T,
                bias.reshape(1, HID_DEV),
                tile_values.reshape(PER_OFFSET, REACH, BLOCK, BLOCK),
                tile_src,
                tile_dst,
                tile_counts,
                out_grad.T,
            )
        )
    )
    out, wg, bg, ig = pl.pallas_call(
        finish,
        out_shape=shapes,
        in_specs=[anywhere] * 4,
        out_specs=(hbm,) * 4,
        scratch_shapes=[dma((4,))],
        compiler_params=pltpu.CompilerParams(vmem_limit_bytes=1024 * 1024),
        name="store_outputs",
    )(*results)
    return out.T, wg.T, bg.reshape(HID_DEV), ig.T


def solution(mesh):
    return jax.shard_map(
        shards,
        mesh=mesh,
        in_specs=(
            P("dom", None),
            P(None, "feat"),
            P("feat"),
            P("dom", None, None),
            P("dom"),
            P("dom"),
            P("dom"),
            P("dom", "feat"),
        ),
        out_specs=(P("dom", "feat"), P(None, "feat"), P("feat"), P("dom", "feat")),
        check_vma=False,
    )
```

time: 57.7 us -> 44.1 us (0.76)
  Pallas kernels: 50.8 us -> 42.7 us
  local copies, waits for them, and re-layouts: 5.28 us -> 0 us
    pallas_call x1 -> x2, Pallas kernels: 50.8 us -> 42.7 us  [the longest x1 42 us: shards(): pl.pallas_call(functools.partial(kernel, n_dom), out_shape=shapes, in_spe...]
    unnamed x4 -> x0, local copies, waits for them, and re-layouts: 5.28 us -> none
where the time goes in v2:
time: 44.1 us; the launch traced here: 44 us
  Pallas kernels  42.7 us (97%)
  between operations  1.29 us (3%)
    pallas_call x1, Pallas kernels, shards(): pl.pallas_call(functools.partial(kernel, n_dom), out_shape=shapes, in_spe...  42 us

profile of v2, /device:TPU:1, one launch (start us, length us, event | category | flops | bytes accessed | tf_op | source)
XLA Modules:
  0.0 44.0 jit_solution(17801741961838043570)
XLA Ops:
  1.3 42.0 %graph_layer.1 = (bf16[32,1024]{1,0:T(8,128)(2,1)S(1)}, f32[32,128]{1,0:T(8,128)S(1)}, f32[1,32]{1,0:T(1,128)S(1)}, bf16[16,1024]{1,0:T(8,128)(2,1)S(1)}) custom-call(bf16[1024,128]{1,0:T(8,128)(2,1)} %nf_hbm.1, bf16[32,128]{1,0:T(8,128)(2,1)} %bitcast.10, f32[1,32]{1,0:T(1,128)} %bitcast.11, bf16[24,4,128,128]{3,2,1,0:T(8,128)(2,1)} %bitcast.8, s32[96]{0:T(128)} %src_hbm.1, ...), custom_call_target="tpu_custom_call" | custom-call | tf_op jit(solution)/shard_map/graph_layer/pallas_call | solution.py:297
  43.3 0.7 %store_outputs.1 = (bf16[32,1024]{1,0:T(8,128)(2,1)}, f32[32,128]{1,0:T(8,128)}, f32[1,32]{1,0:T(1,128)}, bf16[16,1024]{1,0:T(8,128)(2,1)}) custom-call(bf16[32,1024]{1,0:T(8,128)(2,1)S(1)} %get-tuple-element.12.refs_0_, f32[32,128]{1,0:T(8,128)S(1)} %get-tuple-element.13.refs_1_, f32[1,32]{1,0:T(1,128)S(1)} %get-tuple-element.14.refs_2_, ...), custom_call_target="tpu_custom_call" | custom-call | tf_op jit(solution)/shard_map/store_outputs/pallas_call | solution.py:362

commit v3 on v2

--- a/solution.py
+++ b/solution.py
@@ -19,6 +19,7 @@
 F32 = jnp.float32
 BF16 = jnp.bfloat16
 ORDER = (3, 2, 1, 0)
+HOPS = ((2, 1), (1, 1), (3, 1), (2, 0), (1, 0), (3, 0), (0, 1))
 
 
 def kernel(
@@ -27,8 +28,8 @@
     out, wg, bg, ig,
     nf, og, wt, bias, src, dst, tiles, nft, table, psend, precv, agg, hsend, hrecv,
     hall0, hall1, hall2, hall3,
-    rsend, rrecv, rbias, ysend, yrecv, ybias, zbuf, zbias, wfin,
-    load_sem, tile_sem, p_sem, a_sem, h_sem, b_sem, r_sem, y_sem, z_sem, zb_sem, w_sem,
+    rsend, rrecv, rbias, zbuf, zbias, gbuf, gbias,
+    load_sem, tile_sem, p_sem, a_sem, h_sem, b_sem, r_sem, z_sem, zb_sem, g_sem, gb_sem,
     relay_sem,
 ):
     n_z = n_dom // GROUP
@@ -39,13 +40,12 @@
     lane = lax.rem(dom, GROUP)
     core = lax.rem(dom, 2)
     partner = (dom + 1 - 2 * core, feat)
-    across = (z * GROUP + lax.rem(lane + 2, GROUP), feat)
 
     def dom_at(step):
         return lax.rem(dom + (step % n_dom), n_dom)
 
-    def feat_at(step):
-        return lax.rem(feat + step, NFEAT)
+    def feat_at(hop):
+        return lax.rem(feat // 2 + hop[0], NFEAT // 2) * 2 + lax.rem(feat + hop[1], 2)
 
     def z_at(step):
         return lax.rem(z + step, n_z)
@@ -53,6 +53,9 @@
     def z_peer(step):
         return (z_at(step) * GROUP + lane, feat)
 
+    def group_peer(step):
+        return (z * GROUP + lax.rem(lane + step, GROUP), feat)
+
     def around(*distances):
         return sorted({d % n_z for r in distances for d in (r, -r)} - {0})
 
@@ -63,7 +66,7 @@
 
     near = [(dom_at(step), feat) for step in range(1, REACH)]
     near += [(dom_at(-step), feat) for step in range(1, REACH)]
-    near += [(dom, feat_at(step)) for step in range(1, NFEAT)]
+    near += [(dom, feat_at(hop)) for hop in HOPS]
     near += [z_peer(step) for step in around(1, 2)]
     for device in near:
         signal(barrier, device)
@@ -141,15 +144,15 @@
     for o in ORDER[:-1]:
         tile_loads[o].wait()
         psend[o - 1] = forward(o).astype(BF16)
-    tile_loads[0].wait()
-    own = forward(0)
-    for load in loads[3:]:
-        load.wait()
     pl.semaphore_wait(barrier, len(near))
     for o in ORDER[:-1]:
         send(psend.at[o - 1], precv.at[o - 1], p_sem, o - 1, o - 1, (dom_at(o), feat))
     for step in around(2):
         signal(relay_sem.at[0], z_peer(step))
+    tile_loads[0].wait()
+    own = forward(0)
+    for load in loads[3:]:
+        load.wait()
     bias_square = jnp.broadcast_to(bias[...], (HID_DEV, HID_DEV))
     on_diagonal = lax.broadcasted_iota(jnp.int32, (HID_DEV, HID_DEV), 0) == (
         lax.broadcasted_iota(jnp.int32, (HID_DEV, HID_DEV), 1)
@@ -159,14 +162,14 @@
         arrival(precv.at[o - 1], p_sem, o - 1)
         own = own + precv[o - 1].astype(F32)
     agg[feat] = own.astype(BF16)
-    for step in range(1, NFEAT):
-        send(agg.at[feat], agg.at[feat], a_sem, step, feat, (dom, feat_at(step)))
+    for i, hop in enumerate(HOPS):
+        send(agg.at[feat], agg.at[feat], a_sem, i, feat, (dom, feat_at(hop)))
     if around(2):
         pl.semaphore_wait(relay_sem.at[0], len(around(2)))
     for step in around(4):
         signal(relay_sem.at[1], z_peer(step))
-    for step in range(1, NFEAT):
-        arrival(agg.at[feat_at(step)], a_sem, feat_at(step))
+    for hop in HOPS:
+        arrival(agg.at[feat_at(hop)], a_sem, feat_at(hop))
     aggregated = jnp.concatenate(
         [
             jnp.concatenate([agg[i, g * FW : (g + 1) * FW, :] for i in range(NFEAT)], axis=0)
@@ -203,29 +206,24 @@
             hsend[i, g * FW : (g + 1) * FW, :] = back[
                 i * FW : (i + 1) * FW, g * BLOCK : (g + 1) * BLOCK
             ]
-    for step in range(1, NFEAT):
-        send(hsend.at[feat_at(step)], hrecv.at[feat], h_sem, step, feat, (dom, feat_at(step)))
+    for i, hop in enumerate(HOPS):
+        send(hsend.at[feat_at(hop)], hrecv.at[feat], h_sem, i, feat, (dom, feat_at(hop)))
     hrecv[feat] = hsend[feat]
 
+    if around(4):
+        pl.semaphore_wait(relay_sem.at[1], len(around(4)))
     arrival(rrecv, r_sem, 0)
     arrival(rbias.at[1], r_sem, 1)
-    ysend[...] = rsend[core] + rrecv[...]
-    ybias[0] = rbias[0] + rbias[1]
-    send(ysend, yrecv, y_sem, 0, 0, across)
-    send(ybias.at[0], ybias.at[1], y_sem, 1, 1, across)
-    out[...] = (pre * sigmoid_pre).astype(BF16)
-    if around(4):
-        pl.semaphore_wait(relay_sem.at[1], len(around(4)))
-    arrival(yrecv, y_sem, 0)
-    arrival(ybias.at[1], y_sem, 1)
-    zbuf[z] = (ysend[...] + yrecv[...]).astype(BF16)
-    zbias[z] = ybias[0] + ybias[1]
-    for step in range(1, n_z):
+    zbuf[z] = (rsend[core] + rrecv[...]).astype(BF16)
+    zbias[z] = rbias[0] + rbias[1]
+    far_first = sorted(range(1, n_z), key=lambda step: -min(step, n_z - step))
+    for step in far_first:
         send(zbuf.at[z], zbuf.at[z], z_sem, step, z, z_peer(step))
         send(zbias.at[z], zbias.at[z], zb_sem, step, z, z_peer(step))
-
-    for step in range(1, NFEAT):
-        arrival(hrecv.at[feat_at(step)], h_sem, feat_at(step))
+    out[...] = (pre * sigmoid_pre).astype(BF16)
+
+    for hop in HOPS:
+        arrival(hrecv.at[feat_at(hop)], h_sem, feat_at(hop))
     mixed = hrecv[0].astype(F32)
     for i in range(1, NFEAT):
         mixed = mixed + hrecv[i].astype(F32)
@@ -247,6 +245,16 @@
         )
 
     total = backward(0)
+    for step in far_first[::-1]:
+        arrival(zbuf.at[z_at(step)], z_sem, z_at(step))
+    gbuf[lane] = jnp.sum(zbuf[...].astype(F32), axis=0)
+    for step in range(1, GROUP):
+        send(gbuf.at[lane], gbuf.at[lane], g_sem, step, lane, group_peer(step))
+    for step in far_first[::-1]:
+        arrival(zbias.at[z_at(step)], zb_sem, z_at(step))
+    gbias[lane] = jnp.sum(zbias[...], axis=0)
+    for step in range(1, GROUP):
+        send(gbias.at[lane], gbias.at[lane], gb_sem, step, lane, group_peer(step))
     for o in (1, 2, 3):
         arrival(hall[o], b_sem, o)
         total = total + backward(o)
@@ -254,16 +262,13 @@
     for g in range(NB):
         ig[:, g * BLOCK : (g + 1) * BLOCK] = total[g * FW : (g + 1) * FW, :]
 
-    for step in range(1, n_z):
-        arrival(zbuf.at[z_at(step)], z_sem, z_at(step))
-    wfin[core] = jnp.sum(zbuf[...].astype(F32), axis=0)
-    send(wfin.at[core], wfin.at[core], w_sem, 0, core, partner)
-    for step in range(1, n_z):
-        arrival(zbias.at[z_at(step)], zb_sem, z_at(step))
-    bg[...] = jnp.sum(zbias[...], axis=0)[:, 0:HID_DEV]
-    arrival(wfin.at[1 - core], w_sem, 1 - core)
-    wg[0:16, :] = wfin[0]
-    wg[16:32, :] = wfin[1]
+    for step in range(1, GROUP):
+        member = lax.rem(lane + step, GROUP)
+        arrival(gbuf.at[member], g_sem, member)
+        arrival(gbias.at[member], gb_sem, member)
+    wg[0:16, :] = gbuf[0] + gbuf[2]
+    wg[16:32, :] = gbuf[1] + gbuf[3]
+    bg[...] = (gbias[0] + gbias[2])[:, 0:HID_DEV]
     for copy in sends:
         copy.wait_send()
 
@@ -321,12 +326,10 @@
             pltpu.VMEM((2, 16, BLOCK), F32),
             pltpu.VMEM((16, BLOCK), F32),
             pltpu.VMEM((2, 1, BLOCK), F32),
-            pltpu.VMEM((16, BLOCK), F32),
-            pltpu.VMEM((16, BLOCK), F32),
-            pltpu.VMEM((2, 1, BLOCK), F32),
             pltpu.VMEM((n_z, 16, BLOCK), BF16),
             pltpu.VMEM((n_z, 1, BLOCK), F32),
-            pltpu.VMEM((2, 16, BLOCK), F32),
+            pltpu.VMEM((GROUP, 16, BLOCK), F32),
+            pltpu.VMEM((GROUP, 1, BLOCK), F32),
             dma((6,)),
             dma((REACH,)),
             dma((2, REACH - 1)),
@@ -334,10 +337,10 @@
             dma((2, NFEAT)),
             dma((2, REACH)),
             dma((2, 2)),
-            dma((2, 2)),
             dma((2, n_z)),
             dma((2, n_z)),
-            dma((2, 2)),
+            dma((2, GROUP)),
+            dma((2, GROUP)),
             pltpu.SemaphoreType.REGULAR((2,)),
         ],
         compiler_params=pltpu.CompilerParams(

time: 44.1 us -> 39.4 us (0.89)
  Pallas kernels: 42.7 us -> 37.9 us
    pallas_call x1, Pallas kernels: 42 us -> 37.3 us  [shards(): pl.pallas_call(functools.partial(kernel, n_dom), out_shape=shapes, in_spe...]
where the time goes in v3:
time: 39.4 us; the launch traced here: 39.2 us
  Pallas kernels  37.9 us (96%)
  between operations  1.29 us (3%)
    pallas_call x1, Pallas kernels, shards(): pl.pallas_call(functools.partial(kernel, n_dom), out_shape=shapes, in_spe...  37.3 us

profile of v3, /device:TPU:1, one launch (start us, length us, event | category | flops | bytes accessed | tf_op | source)
XLA Modules:
  0.0 39.2 jit_solution(8847662566483762054)
XLA Ops:
  1.3 37.3 %graph_layer.1 = (bf16[32,1024]{1,0:T(8,128)(2,1)S(1)}, f32[32,128]{1,0:T(8,128)S(1)}, f32[1,32]{1,0:T(1,128)S(1)}, bf16[16,1024]{1,0:T(8,128)(2,1)S(1)}) custom-call(bf16[1024,128]{1,0:T(8,128)(2,1)} %nf_hbm.1, bf16[32,128]{1,0:T(8,128)(2,1)} %bitcast.10, f32[1,32]{1,0:T(1,128)} %bitcast.11, bf16[24,4,128,128]{3,2,1,0:T(8,128)(2,1)} %bitcast.8, s32[96]{0:T(128)} %src_hbm.1, ...), custom_call_target="tpu_custom_call" | custom-call | tf_op jit(solution)/shard_map/graph_layer/pallas_call | solution.py:302
  38.5 0.7 %store_outputs.1 = (bf16[32,1024]{1,0:T(8,128)(2,1)}, f32[32,128]{1,0:T(8,128)}, f32[1,32]{1,0:T(1,128)}, bf16[16,1024]{1,0:T(8,128)(2,1)}) custom-call(bf16[32,1024]{1,0:T(8,128)(2,1)S(1)} %get-tuple-element.12.refs_0_, f32[32,128]{1,0:T(8,128)S(1)} %get-tuple-element.13.refs_1_, f32[1,32]{1,0:T(1,128)S(1)} %get-tuple-element.14.refs_2_, ...), custom_call_target="tpu_custom_call" | custom-call | tf_op jit(solution)/shard_map/store_outputs/pallas_call | solution.py:365

commit v4 on v3

--- a/solution.py
+++ b/solution.py
@@ -29,7 +29,7 @@
     nf, og, wt, bias, src, dst, tiles, nft, table, psend, precv, agg, hsend, hrecv,
     hall0, hall1, hall2, hall3,
     rsend, rrecv, rbias, zbuf, zbias, gbuf, gbias,
-    load_sem, tile_sem, p_sem, a_sem, h_sem, b_sem, r_sem, z_sem, zb_sem, g_sem, gb_sem,
+    load_sem, tile_sem, p_sem, a_sem, h_sem, b_sem, r_sem, rb_sem, z_sem, zb_sem, g_sem, gb_sem,
     relay_sem,
 ):
     n_z = n_dom // GROUP
@@ -87,22 +87,21 @@
     for load in loads[3:]:
         load.start()
 
-    sends = []
-
-    def send(src_ref, dst_ref, sems, s, r, device):
-        copy = pltpu.make_async_remote_copy(
+    def send(src_ref, dst_ref, sems, device, r=1):
+        pltpu.make_async_remote_copy(
             src_ref=src_ref,
             dst_ref=dst_ref,
-            send_sem=sems.at[0, s],
-            recv_sem=sems.at[1, r],
+            send_sem=sems.at[0],
+            recv_sem=sems.at[r],
             device_id=device,
             device_id_type=MESH,
-        )
-        copy.start()
-        sends.append(copy)
-
-    def arrival(ref, sems, r):
-        pltpu.make_async_copy(ref, ref, sems.at[1, r]).wait()
+        ).start()
+
+    def sent(ref, sems):
+        pltpu.make_async_copy(ref, ref, sems.at[0]).wait()
+
+    def arrival(ref, sems, r=1):
+        pltpu.make_async_copy(ref, ref, sems.at[r]).wait()
 
     one = jnp.ones((FW, BLOCK), BF16)
     zero = jnp.zeros((FW, BLOCK), BF16)
@@ -146,7 +145,7 @@
         psend[o - 1] = forward(o).astype(BF16)
     pl.semaphore_wait(barrier, len(near))
     for o in ORDER[:-1]:
-        send(psend.at[o - 1], precv.at[o - 1], p_sem, o - 1, o - 1, (dom_at(o), feat))
+        send(psend.at[o - 1], precv.at[o - 1], p_sem, (dom_at(o), feat))
     for step in around(2):
         signal(relay_sem.at[0], z_peer(step))
     tile_loads[0].wait()
@@ -158,18 +157,17 @@
         lax.broadcasted_iota(jnp.int32, (HID_DEV, HID_DEV), 1)
     )
     bias_column = jnp.sum(jnp.where(on_diagonal, bias_square, 0.0), axis=1, keepdims=True)
+    arrival(precv, p_sem)
     for o in ORDER[:-1]:
-        arrival(precv.at[o - 1], p_sem, o - 1)
         own = own + precv[o - 1].astype(F32)
     agg[feat] = own.astype(BF16)
-    for i, hop in enumerate(HOPS):
-        send(agg.at[feat], agg.at[feat], a_sem, i, feat, (dom, feat_at(hop)))
+    for hop in HOPS:
+        send(agg.at[feat], agg.at[feat], a_sem, (dom, feat_at(hop)))
     if around(2):
         pl.semaphore_wait(relay_sem.at[0], len(around(2)))
     for step in around(4):
         signal(relay_sem.at[1], z_peer(step))
-    for hop in HOPS:
-        arrival(agg.at[feat_at(hop)], a_sem, feat_at(hop))
+    arrival(agg.at[0 : NFEAT - 1], a_sem)
     aggregated = jnp.concatenate(
         [
             jnp.concatenate([agg[i, g * FW : (g + 1) * FW, :] for i in range(NFEAT)], axis=0)
@@ -195,8 +193,8 @@
     rsend[0] = weight_part[0:16, :]
     rsend[1] = weight_part[16:32, :]
     rbias[0] = bias_part[0:1, :]
-    send(rsend.at[1 - core], rrecv, r_sem, 0, 0, partner)
-    send(rbias.at[0], rbias.at[1], r_sem, 1, 1, partner)
+    send(rsend.at[1 - core], rrecv, r_sem, partner)
+    send(rbias.at[0], rbias.at[1], rb_sem, partner)
 
     back = lax.dot_general(
         wt[...], grad_pre, (((0,), (0,)), ((), ())), preferred_element_type=F32
@@ -206,24 +204,23 @@
             hsend[i, g * FW : (g + 1) * FW, :] = back[
                 i * FW : (i + 1) * FW, g * BLOCK : (g + 1) * BLOCK
             ]
-    for i, hop in enumerate(HOPS):
-        send(hsend.at[feat_at(hop)], hrecv.at[feat], h_sem, i, feat, (dom, feat_at(hop)))
+    for hop in HOPS:
+        send(hsend.at[feat_at(hop)], hrecv.at[feat], h_sem, (dom, feat_at(hop)))
     hrecv[feat] = hsend[feat]
 
     if around(4):
         pl.semaphore_wait(relay_sem.at[1], len(around(4)))
-    arrival(rrecv, r_sem, 0)
-    arrival(rbias.at[1], r_sem, 1)
+    arrival(rrecv, r_sem)
+    arrival(rbias.at[1], rb_sem)
     zbuf[z] = (rsend[core] + rrecv[...]).astype(BF16)
     zbias[z] = rbias[0] + rbias[1]
     far_first = sorted(range(1, n_z), key=lambda step: -min(step, n_z - step))
     for step in far_first:
-        send(zbuf.at[z], zbuf.at[z], z_sem, step, z, z_peer(step))
-        send(zbias.at[z], zbias.at[z], zb_sem, step, z, z_peer(step))
+        send(zbuf.at[z], zbuf.at[z], z_sem, z_peer(step))
+        send(zbias.at[z], zbias.at[z], zb_sem, z_peer(step))
     out[...] = (pre * sigmoid_pre).astype(BF16)
 
-    for hop in HOPS:
-        arrival(hrecv.at[feat_at(hop)], h_sem, feat_at(hop))
+    arrival(hrecv.at[0 : NFEAT - 1], h_sem)
     mixed = hrecv[0].astype(F32)
     for i in range(1, NFEAT):
         mixed = mixed + hrecv[i].astype(F32)
@@ -231,7 +228,7 @@
     for g in range(NB):
         hall0[g] = mixed[g * FW : (g + 1) * FW, :]
     for o in ORDER[:-1]:
-        send(hall0, hall[o], b_sem, o, o, (dom_at(-o), feat))
+        send(hall0, hall[o], b_sem, (dom_at(-o), feat), o)
 
     def backward(o):
         left = []
@@ -245,16 +242,14 @@
         )
 
     total = backward(0)
-    for step in far_first[::-1]:
-        arrival(zbuf.at[z_at(step)], z_sem, z_at(step))
+    arrival(zbuf.at[0 : n_z - 1], z_sem)
     gbuf[lane] = jnp.sum(zbuf[...].astype(F32), axis=0)
     for step in range(1, GROUP):
-        send(gbuf.at[lane], gbuf.at[lane], g_sem, step, lane, group_peer(step))
-    for step in far_first[::-1]:
-        arrival(zbias.at[z_at(step)], zb_sem, z_at(step))
+        send(gbuf.at[lane], gbuf.at[lane], g_sem, group_peer(step))
+    arrival(zbias.at[0 : n_z - 1], zb_sem)
     gbias[lane] = jnp.sum(zbias[...], axis=0)
     for step in range(1, GROUP):
-        send(gbias.at[lane], gbias.at[lane], gb_sem, step, lane, group_peer(step))
+        send(gbias.at[lane], gbias.at[lane], gb_sem, group_peer(step))
     for o in (1, 2, 3):
         arrival(hall[o], b_sem, o)
         total = total + backward(o)
@@ -262,15 +257,21 @@
     for g in range(NB):
         ig[:, g * BLOCK : (g + 1) * BLOCK] = total[g * FW : (g + 1) * FW, :]
 
-    for step in range(1, GROUP):
-        member = lax.rem(lane + step, GROUP)
-        arrival(gbuf.at[member], g_sem, member)
-        arrival(gbias.at[member], gb_sem, member)
+    arrival(gbuf.at[0 : GROUP - 1], g_sem)
+    arrival(gbias.at[0 : GROUP - 1], gb_sem)
     wg[0:16, :] = gbuf[0] + gbuf[2]
     wg[16:32, :] = gbuf[1] + gbuf[3]
     bg[...] = (gbias[0] + gbias[2])[:, 0:HID_DEV]
-    for copy in sends:
-        copy.wait_send()
+    sent(psend, p_sem)
+    sent(agg.at[0 : NFEAT - 1], a_sem)
+    sent(rsend.at[0], r_sem)
+    sent(rbias.at[0], rb_sem)
+    sent(hsend.at[0 : NFEAT - 1], h_sem)
+    sent(zbuf.at[0 : n_z - 1], z_sem)
+    sent(zbias.at[0 : n_z - 1], zb_sem)
+    sent(psend, b_sem)
+    sent(gbuf.at[0 : GROUP - 1], g_sem)
+    sent(gbias.at[0 : GROUP - 1], gb_sem)
 
 
 def finish(*refs):
@@ -332,15 +333,16 @@
             pltpu.VMEM((GROUP, 1, BLOCK), F32),
             dma((6,)),
             dma((REACH,)),
-            dma((2, REACH - 1)),
-            dma((2, NFEAT)),
-            dma((2, NFEAT)),
-            dma((2, REACH)),
-            dma((2, 2)),
-            dma((2, n_z)),
-            dma((2, n_z)),
-            dma((2, GROUP)),
-            dma((2, GROUP)),
+            dma((2,)),
+            dma((2,)),
+            dma((2,)),
+            dma((REACH,)),
+            dma((2,)),
+            dma((2,)),
+            dma((2,)),
+            dma((2,)),
+            dma((2,)),
+            dma((2,)),
             pltpu.SemaphoreType.REGULAR((2,)),
         ],
         compiler_params=pltpu.CompilerParams(

time: 39.4 us -> 38.6 us (0.980)
  Pallas kernels: 37.9 us -> 37.2 us
    pallas_call x1, Pallas kernels: 37.3 us -> 36.5 us  [shards(): pl.pallas_call(functools.partial(kernel, n_dom), out_shape=shapes, in_spe...]
where the time goes in v4:
time: 38.6 us; the launch traced here: 38.5 us
  Pallas kernels  37.2 us (96%)
  between operations  1.29 us (3%)
    pallas_call x1, Pallas kernels, shards(): pl.pallas_call(functools.partial(kernel, n_dom), out_shape=shapes, in_spe...  36.5 us

profile of v4, /device:TPU:1, one launch (start us, length us, event | category | flops | bytes accessed | tf_op | source)
XLA Modules:
  0.0 38.5 jit_solution(7901617040196996744)
XLA Ops:
  1.3 36.5 %graph_layer.1 = (bf16[32,1024]{1,0:T(8,128)(2,1)S(1)}, f32[32,128]{1,0:T(8,128)S(1)}, f32[1,32]{1,0:T(1,128)S(1)}, bf16[16,1024]{1,0:T(8,128)(2,1)S(1)}) custom-call(bf16[1024,128]{1,0:T(8,128)(2,1)} %nf_hbm.1, bf16[32,128]{1,0:T(8,128)(2,1)} %bitcast.10, f32[1,32]{1,0:T(1,128)} %bitcast.11, bf16[24,4,128,128]{3,2,1,0:T(8,128)(2,1)} %bitcast.8, s32[96]{0:T(128)} %src_hbm.1, ...), custom_call_target="tpu_custom_call" | custom-call | tf_op jit(solution)/shard_map/graph_layer/pallas_call | solution.py:303
  37.8 0.7 %store_outputs.1 = (bf16[32,1024]{1,0:T(8,128)(2,1)}, f32[32,128]{1,0:T(8,128)}, f32[1,32]{1,0:T(1,128)}, bf16[16,1024]{1,0:T(8,128)(2,1)}) custom-call(bf16[32,1024]{1,0:T(8,128)(2,1)S(1)} %get-tuple-element.12.refs_0_, f32[32,128]{1,0:T(8,128)S(1)} %get-tuple-element.13.refs_1_, f32[1,32]{1,0:T(1,128)S(1)} %get-tuple-element.14.refs_2_, ...), custom_call_target="tpu_custom_call" | custom-call | tf_op jit(solution)/shard_map/store_outputs/pallas_call | solution.py:367

commit v5 on v4

--- a/solution.py
+++ b/solution.py
@@ -13,6 +13,8 @@
 NFEAT = 8
 FW = 16
 PER_OFFSET = 24
+HALVES = (0, 1)
+HALF = 64
 HID_DEV = 32
 GROUP = 4
 MESH = pl.DeviceIdType.MESH
@@ -142,10 +144,15 @@
 
     for o in ORDER[:-1]:
         tile_loads[o].wait()
-        psend[o - 1] = forward(o).astype(BF16)
+        part = forward(o).astype(BF16)
+        for half in HALVES:
+            psend[half, o - 1] = part[half * HALF : (half + 1) * HALF, :]
     pl.semaphore_wait(barrier, len(near))
-    for o in ORDER[:-1]:
-        send(psend.at[o - 1], precv.at[o - 1], p_sem, (dom_at(o), feat))
+    for half in HALVES:
+        for o in ORDER[:-1]:
+            send(
+                psend.at[half, o - 1], precv.at[half, o - 1], p_sem, (dom_at(o), feat), 1 + half
+            )
     for step in around(2):
         signal(relay_sem.at[0], z_peer(step))
     tile_loads[0].wait()
@@ -157,56 +164,75 @@
         lax.broadcasted_iota(jnp.int32, (HID_DEV, HID_DEV), 1)
     )
     bias_column = jnp.sum(jnp.where(on_diagonal, bias_square, 0.0), axis=1, keepdims=True)
-    arrival(precv, p_sem)
-    for o in ORDER[:-1]:
-        own = own + precv[o - 1].astype(F32)
-    agg[feat] = own.astype(BF16)
-    for hop in HOPS:
-        send(agg.at[feat], agg.at[feat], a_sem, (dom, feat_at(hop)))
+    for half in HALVES:
+        arrival(precv.at[half], p_sem, 1 + half)
+        piece = own[half * HALF : (half + 1) * HALF, :]
+        for o in ORDER[:-1]:
+            piece = piece + precv[half, o - 1].astype(F32)
+        agg[half, feat] = piece.astype(BF16)
+        for hop in HOPS:
+            send(
+                agg.at[half, feat], agg.at[half, feat], a_sem, (dom, feat_at(hop)), 1 + half
+            )
     if around(2):
         pl.semaphore_wait(relay_sem.at[0], len(around(2)))
     for step in around(4):
         signal(relay_sem.at[1], z_peer(step))
-    arrival(agg.at[0 : NFEAT - 1], a_sem)
-    aggregated = jnp.concatenate(
-        [
-            jnp.concatenate([agg[i, g * FW : (g + 1) * FW, :] for i in range(NFEAT)], axis=0)
-            for g in range(NB)
-        ],
-        axis=1,
-    )
-    pre = jnp.dot(wt[...], aggregated, preferred_element_type=F32) + bias_column
-    sigmoid_pre = jax.nn.sigmoid(pre)
-    grad_pre = (
-        og[...].astype(F32) * sigmoid_pre * (1.0 + pre * (1.0 - sigmoid_pre))
-    ).astype(BF16)
-
-    weight_part = lax.dot_general(
-        grad_pre, aggregated, (((1,), (1,)), ((), ())), preferred_element_type=F32
-    )
-    bias_part = lax.dot_general(
-        jnp.ones((8, NB * BLOCK), BF16),
-        jnp.concatenate([grad_pre] * 4, axis=0),
-        (((1,), (1,)), ((), ())),
-        preferred_element_type=F32,
-    )
+
+    def send_back(grad_pre, half):
+        back = lax.dot_general(
+            wt[...], grad_pre, (((0,), (0,)), ((), ())), preferred_element_type=F32
+        ).astype(BF16)
+        for i in range(NFEAT):
+            for g in range(NB // 2):
+                hsend[half, i, g * FW : (g + 1) * FW, :] = back[
+                    i * FW : (i + 1) * FW, g * BLOCK : (g + 1) * BLOCK
+                ]
+        for hop in HOPS:
+            send(
+                hsend.at[half, feat_at(hop)], hrecv.at[half, feat], h_sem,
+                (dom, feat_at(hop)), 1 + half,
+            )
+        hrecv[half, feat] = hsend[half, feat]
+
+    weight_part = jnp.zeros((HID_DEV, BLOCK), F32)
+    bias_part = jnp.zeros((8, BLOCK), F32)
+    for half in HALVES:
+        arrival(agg.at[half, 0 : NFEAT - 1], a_sem, 1 + half)
+        aggregated = jnp.concatenate(
+            [
+                jnp.concatenate(
+                    [agg[half, i, g * FW : (g + 1) * FW, :] for i in range(NFEAT)], axis=0
+                )
+                for g in range(NB // 2)
+            ],
+            axis=1,
+        )
+        nodes = slice(half * NB // 2 * BLOCK, (half + 1) * NB // 2 * BLOCK)
+        pre = jnp.dot(wt[...], aggregated, preferred_element_type=F32) + bias_column
+        sigmoid_pre = jax.nn.sigmoid(pre)
+        grad_pre = (
+            og[:, nodes].astype(F32) * sigmoid_pre * (1.0 + pre * (1.0 - sigmoid_pre))
+        ).astype(BF16)
+        if half == 0:
+            send_back(grad_pre, half)
+        out[:, nodes] = (pre * sigmoid_pre).astype(BF16)
+        weight_part = weight_part + lax.dot_general(
+            grad_pre, aggregated, (((1,), (1,)), ((), ())), preferred_element_type=F32
+        )
+        bias_part = bias_part + lax.dot_general(
+            jnp.ones((8, NB // 2 * BLOCK), BF16),
+            jnp.concatenate([grad_pre] * 4, axis=0),
+            (((1,), (1,)), ((), ())),
+            preferred_element_type=F32,
+        )
     rsend[0] = weight_part[0:16, :]
     rsend[1] = weight_part[16:32, :]
     rbias[0] = bias_part[0:1, :]
     send(rsend.at[1 - core], rrecv, r_sem, partner)
     send(rbias.at[0], rbias.at[1], rb_sem, partner)
 
-    back = lax.dot_general(
-        wt[...], grad_pre, (((0,), (0,)), ((), ())), preferred_element_type=F32
-    ).astype(BF16)
-    for i in range(NFEAT):
-        for g in range(NB):
-            hsend[i, g * FW : (g + 1) * FW, :] = back[
-                i * FW : (i + 1) * FW, g * BLOCK : (g + 1) * BLOCK
-            ]
-    for hop in HOPS:
-        send(hsend.at[feat_at(hop)], hrecv.at[feat], h_sem, (dom, feat_at(hop)))
-    hrecv[feat] = hsend[feat]
+    send_back(grad_pre, 1)
 
     if around(4):
         pl.semaphore_wait(relay_sem.at[1], len(around(4)))
@@ -218,17 +244,19 @@
     for step in far_first:
         send(zbuf.at[z], zbuf.at[z], z_sem, z_peer(step))
         send(zbias.at[z], zbias.at[z], zb_sem, z_peer(step))
-    out[...] = (pre * sigmoid_pre).astype(BF16)
-
-    arrival(hrecv.at[0 : NFEAT - 1], h_sem)
-    mixed = hrecv[0].astype(F32)
-    for i in range(1, NFEAT):
-        mixed = mixed + hrecv[i].astype(F32)
-    mixed = mixed.astype(BF16)
-    for g in range(NB):
-        hall0[g] = mixed[g * FW : (g + 1) * FW, :]
-    for o in ORDER[:-1]:
-        send(hall0, hall[o], b_sem, (dom_at(-o), feat), o)
+
+    for half in HALVES:
+        arrival(hrecv.at[half, 0 : NFEAT - 1], h_sem, 1 + half)
+        mixed = hrecv[half, 0].astype(F32)
+        for i in range(1, NFEAT):
+            mixed = mixed + hrecv[half, i].astype(F32)
+        mixed = mixed.astype(BF16)
+        first = half * NB // 2
+        for g in range(NB // 2):
+            hall0[first + g] = mixed[g * FW : (g + 1) * FW, :]
+        blocks = pl.ds(first, NB // 2)
+        for o in ORDER[:-1]:
+            send(hall0.at[blocks], hall[o].at[blocks], b_sem, (dom_at(-o), feat), o)
 
     def backward(o):
         left = []
@@ -263,10 +291,10 @@
     wg[16:32, :] = gbuf[1] + gbuf[3]
     bg[...] = (gbias[0] + gbias[2])[:, 0:HID_DEV]
     sent(psend, p_sem)
-    sent(agg.at[0 : NFEAT - 1], a_sem)
+    sent(agg.at[:, 0 : NFEAT - 1], a_sem)
     sent(rsend.at[0], r_sem)
     sent(rbias.at[0], rb_sem)
-    sent(hsend.at[0 : NFEAT - 1], h_sem)
+    sent(hsend.at[:, 0 : NFEAT - 1], h_sem)
     sent(zbuf.at[0 : n_z - 1], z_sem)
     sent(zbias.at[0 : n_z - 1], zb_sem)
     sent(psend, b_sem)
@@ -292,7 +320,7 @@
     anywhere = pl.BlockSpec(memory_space=pl.ANY)
     dma = pltpu.SemaphoreType.DMA
     block = pltpu.VMEM((NB, FW, BLOCK), BF16)
-    square = pltpu.VMEM((NFEAT, BLOCK, BLOCK), BF16)
+    square = pltpu.VMEM((2, NFEAT, HALF, BLOCK), BF16)
     limit = 24 * 1024 * 1024
     shapes = (
         jax.ShapeDtypeStruct((HID_DEV, nodes), BF16),
@@ -315,8 +343,8 @@
             pltpu.VMEM((REACH, PER_OFFSET, BLOCK, BLOCK), BF16),
             block,
             pltpu.VMEM((NB + 1, BLOCK, BLOCK), BF16),
-            pltpu.VMEM((REACH - 1, BLOCK, BLOCK), BF16),
-            pltpu.VMEM((REACH - 1, BLOCK, BLOCK), BF16),
+            pltpu.VMEM((2, REACH - 1, HALF, BLOCK), BF16),
+            pltpu.VMEM((2, REACH - 1, HALF, BLOCK), BF16),
             square,
             square,
             square,
@@ -333,9 +361,9 @@
             pltpu.VMEM((GROUP, 1, BLOCK), F32),
             dma((6,)),
             dma((REACH,)),
-            dma((2,)),
-            dma((2,)),
-            dma((2,)),
+            dma((3,)),
+            dma((3,)),
+            dma((3,)),
             dma((REACH,)),
             dma((2,)),
             dma((2,)),

time: 38.6 us -> 38.4 us (level)
  no operation moved by 1% of the time
where the time goes in v5:
time: 38.4 us; the launch traced here: 38.3 us
  Pallas kernels  37 us (96%)
  between operations  1.29 us (3%)
    pallas_call x1, Pallas kernels, shards(): pl.pallas_call(functools.partial(kernel, n_dom), out_shape=shapes, in_spe...  36.3 us

profile of v5, /device:TPU:1, one launch (start us, length us, event | category | flops | bytes accessed | tf_op | source)
XLA Modules:
  0.0 38.3 jit_solution(16702995777833238766)
XLA Ops:
  1.3 36.3 %graph_layer.1 = (bf16[32,1024]{1,0:T(8,128)(2,1)S(1)}, f32[32,128]{1,0:T(8,128)S(1)}, f32[1,32]{1,0:T(1,128)S(1)}, bf16[16,1024]{1,0:T(8,128)(2,1)S(1)}) custom-call(bf16[1024,128]{1,0:T(8,128)(2,1)} %nf_hbm.1, bf16[32,128]{1,0:T(8,128)(2,1)} %bitcast.10, f32[1,32]{1,0:T(1,128)} %bitcast.11, bf16[24,4,128,128]{3,2,1,0:T(8,128)(2,1)} %bitcast.8, s32[96]{0:T(128)} %src_hbm.1, ...), custom_call_target="tpu_custom_call" | custom-call | tf_op jit(solution)/shard_map/graph_layer/pallas_call | solution.py:331
  37.6 0.7 %store_outputs.1 = (bf16[32,1024]{1,0:T(8,128)(2,1)}, f32[32,128]{1,0:T(8,128)}, f32[1,32]{1,0:T(1,128)}, bf16[16,1024]{1,0:T(8,128)(2,1)}) custom-call(bf16[32,1024]{1,0:T(8,128)(2,1)S(1)} %get-tuple-element.12.refs_0_, f32[32,128]{1,0:T(8,128)S(1)} %get-tuple-element.13.refs_1_, f32[1,32]{1,0:T(1,128)S(1)} %get-tuple-element.14.refs_2_, ...), custom_call_target="tpu_custom_call" | custom-call | tf_op jit(solution)/shard_map/store_outputs/pallas_call | solution.py:395

commit v6 on v5

--- a/solution.py
+++ b/solution.py
@@ -13,8 +13,9 @@
 NFEAT = 8
 FW = 16
 PER_OFFSET = 24
-HALVES = (0, 1)
-HALF = 64
+PIECES = (0, 1, 2, 3)
+ROWS = 32
+SPAN = 2
 HID_DEV = 32
 GROUP = 4
 MESH = pl.DeviceIdType.MESH
@@ -145,13 +146,13 @@
     for o in ORDER[:-1]:
         tile_loads[o].wait()
         part = forward(o).astype(BF16)
-        for half in HALVES:
-            psend[half, o - 1] = part[half * HALF : (half + 1) * HALF, :]
+        for part_no in PIECES:
+            psend[part_no, o - 1] = part[part_no * ROWS : (part_no + 1) * ROWS, :]
     pl.semaphore_wait(barrier, len(near))
-    for half in HALVES:
+    for part_no in PIECES:
         for o in ORDER[:-1]:
             send(
-                psend.at[half, o - 1], precv.at[half, o - 1], p_sem, (dom_at(o), feat), 1 + half
+                psend.at[part_no, o - 1], precv.at[part_no, o - 1], p_sem, (dom_at(o), feat), 1 + part_no
             )
     for step in around(2):
         signal(relay_sem.at[0], z_peer(step))
@@ -164,64 +165,64 @@
         lax.broadcasted_iota(jnp.int32, (HID_DEV, HID_DEV), 1)
     )
     bias_column = jnp.sum(jnp.where(on_diagonal, bias_square, 0.0), axis=1, keepdims=True)
-    for half in HALVES:
-        arrival(precv.at[half], p_sem, 1 + half)
-        piece = own[half * HALF : (half + 1) * HALF, :]
+    for part_no in PIECES:
+        arrival(precv.at[part_no], p_sem, 1 + part_no)
+        piece = own[part_no * ROWS : (part_no + 1) * ROWS, :]
         for o in ORDER[:-1]:
-            piece = piece + precv[half, o - 1].astype(F32)
-        agg[half, feat] = piece.astype(BF16)
+            piece = piece + precv[part_no, o - 1].astype(F32)
+        agg[part_no, feat] = piece.astype(BF16)
         for hop in HOPS:
             send(
-                agg.at[half, feat], agg.at[half, feat], a_sem, (dom, feat_at(hop)), 1 + half
+                agg.at[part_no, feat], agg.at[part_no, feat], a_sem, (dom, feat_at(hop)), 1 + part_no
             )
     if around(2):
         pl.semaphore_wait(relay_sem.at[0], len(around(2)))
     for step in around(4):
         signal(relay_sem.at[1], z_peer(step))
 
-    def send_back(grad_pre, half):
+    def send_back(grad_pre, part_no):
         back = lax.dot_general(
             wt[...], grad_pre, (((0,), (0,)), ((), ())), preferred_element_type=F32
         ).astype(BF16)
         for i in range(NFEAT):
-            for g in range(NB // 2):
-                hsend[half, i, g * FW : (g + 1) * FW, :] = back[
+            for g in range(SPAN):
+                hsend[part_no, i, g * FW : (g + 1) * FW, :] = back[
                     i * FW : (i + 1) * FW, g * BLOCK : (g + 1) * BLOCK
                 ]
         for hop in HOPS:
             send(
-                hsend.at[half, feat_at(hop)], hrecv.at[half, feat], h_sem,
-                (dom, feat_at(hop)), 1 + half,
+                hsend.at[part_no, feat_at(hop)], hrecv.at[part_no, feat], h_sem,
+                (dom, feat_at(hop)), 1 + part_no,
             )
-        hrecv[half, feat] = hsend[half, feat]
+        hrecv[part_no, feat] = hsend[part_no, feat]
 
     weight_part = jnp.zeros((HID_DEV, BLOCK), F32)
     bias_part = jnp.zeros((8, BLOCK), F32)
-    for half in HALVES:
-        arrival(agg.at[half, 0 : NFEAT - 1], a_sem, 1 + half)
+    for part_no in PIECES:
+        arrival(agg.at[part_no, 0 : NFEAT - 1], a_sem, 1 + part_no)
         aggregated = jnp.concatenate(
             [
                 jnp.concatenate(
-                    [agg[half, i, g * FW : (g + 1) * FW, :] for i in range(NFEAT)], axis=0
+                    [agg[part_no, i, g * FW : (g + 1) * FW, :] for i in range(NFEAT)], axis=0
                 )
-                for g in range(NB // 2)
+                for g in range(SPAN)
             ],
             axis=1,
         )
-        nodes = slice(half * NB // 2 * BLOCK, (half + 1) * NB // 2 * BLOCK)
+        nodes = slice(part_no * SPAN * BLOCK, (part_no + 1) * SPAN * BLOCK)
         pre = jnp.dot(wt[...], aggregated, preferred_element_type=F32) + bias_column
         sigmoid_pre = jax.nn.sigmoid(pre)
         grad_pre = (
             og[:, nodes].astype(F32) * sigmoid_pre * (1.0 + pre * (1.0 - sigmoid_pre))
         ).astype(BF16)
-        if half == 0:
-            send_back(grad_pre, half)
+        if part_no < PIECES[-1]:
+            send_back(grad_pre, part_no)
         out[:, nodes] = (pre * sigmoid_pre).astype(BF16)
         weight_part = weight_part + lax.dot_general(
             grad_pre, aggregated, (((1,), (1,)), ((), ())), preferred_element_type=F32
         )
         bias_part = bias_part + lax.dot_general(
-            jnp.ones((8, NB // 2 * BLOCK), BF16),
+            jnp.ones((8, SPAN * BLOCK), BF16),
             jnp.concatenate([grad_pre] * 4, axis=0),
             (((1,), (1,)), ((), ())),
             preferred_element_type=F32,
@@ -232,7 +233,7 @@
     send(rsend.at[1 - core], rrecv, r_sem, partner)
     send(rbias.at[0], rbias.at[1], rb_sem, partner)
 
-    send_back(grad_pre, 1)
+    send_back(grad_pre, PIECES[-1])
 
     if around(4):
         pl.semaphore_wait(relay_sem.at[1], len(around(4)))
@@ -245,16 +246,16 @@
         send(zbuf.at[z], zbuf.at[z], z_sem, z_peer(step))
         send(zbias.at[z], zbias.at[z], zb_sem, z_peer(step))
 
-    for half in HALVES:
-        arrival(hrecv.at[half, 0 : NFEAT - 1], h_sem, 1 + half)
-        mixed = hrecv[half, 0].astype(F32)
+    for part_no in PIECES:
+        arrival(hrecv.at[part_no, 0 : NFEAT - 1], h_sem, 1 + part_no)
+        mixed = hrecv[part_no, 0].astype(F32)
         for i in range(1, NFEAT):
-            mixed = mixed + hrecv[half, i].astype(F32)
+            mixed = mixed + hrecv[part_no, i].astype(F32)
         mixed = mixed.astype(BF16)
-        first = half * NB // 2
-        for g in range(NB // 2):
+        first = part_no * SPAN
+        for g in range(SPAN):
             hall0[first + g] = mixed[g * FW : (g + 1) * FW, :]
-        blocks = pl.ds(first, NB // 2)
+        blocks = pl.ds(first, SPAN)
         for o in ORDER[:-1]:
             send(hall0.at[blocks], hall[o].at[blocks], b_sem, (dom_at(-o), feat), o)
 
@@ -320,7 +321,7 @@
     anywhere = pl.BlockSpec(memory_space=pl.ANY)
     dma = pltpu.SemaphoreType.DMA
     block = pltpu.VMEM((NB, FW, BLOCK), BF16)
-    square = pltpu.VMEM((2, NFEAT, HALF, BLOCK), BF16)
+    square = pltpu.VMEM((len(PIECES), NFEAT, ROWS, BLOCK), BF16)
     limit = 24 * 1024 * 1024
     shapes = (
         jax.ShapeDtypeStruct((HID_DEV, nodes), BF16),
@@ -343,8 +344,8 @@
             pltpu.VMEM((REACH, PER_OFFSET, BLOCK, BLOCK), BF16),
             block,
             pltpu.VMEM((NB + 1, BLOCK, BLOCK), BF16),
-            pltpu.VMEM((2, REACH - 1, HALF, BLOCK), BF16),
-            pltpu.VMEM((2, REACH - 1, HALF, BLOCK), BF16),
+            pltpu.VMEM((len(PIECES), REACH - 1, ROWS, BLOCK), BF16),
+            pltpu.VMEM((len(PIECES), REACH - 1, ROWS, BLOCK), BF16),
             square,
             square,
             square,
@@ -361,9 +362,9 @@
             pltpu.VMEM((GROUP, 1, BLOCK), F32),
             dma((6,)),
             dma((REACH,)),
-            dma((3,)),
-            dma((3,)),
-            dma((3,)),
+            dma((5,)),
+            dma((5,)),
+            dma((5,)),
             dma((REACH,)),
             dma((2,)),
             dma((2,)),

time: 38.4 us -> 38.3 us (level)
  no operation moved by 1% of the time
where the time goes in v6:
time: 38.3 us; the launch traced here: 38.1 us
  Pallas kernels  36.8 us (96%)
  between operations  1.29 us (3%)
    pallas_call x1, Pallas kernels, shards(): pl.pallas_call(functools.partial(kernel, n_dom), out_shape=shapes, in_spe...  36.2 us

profile of v6, /device:TPU:1, one launch (start us, length us, event | category | flops | bytes accessed | tf_op | source)
XLA Modules:
  0.0 38.1 jit_solution(10597219906587861875)
XLA Ops:
  1.3 36.2 %graph_layer.1 = (bf16[32,1024]{1,0:T(8,128)(2,1)S(1)}, f32[32,128]{1,0:T(8,128)S(1)}, f32[1,32]{1,0:T(1,128)S(1)}, bf16[16,1024]{1,0:T(8,128)(2,1)S(1)}) custom-call(bf16[1024,128]{1,0:T(8,128)(2,1)} %nf_hbm.1, bf16[32,128]{1,0:T(8,128)(2,1)} %bitcast.10, f32[1,32]{1,0:T(1,128)} %bitcast.11, bf16[24,4,128,128]{3,2,1,0:T(8,128)(2,1)} %bitcast.8, s32[96]{0:T(128)} %src_hbm.1, ...), custom_call_target="tpu_custom_call" | custom-call | tf_op jit(solution)/shard_map/graph_layer/pallas_call | solution.py:332
  37.5 0.7 %store_outputs.1 = (bf16[32,1024]{1,0:T(8,128)(2,1)}, f32[32,128]{1,0:T(8,128)}, f32[1,32]{1,0:T(1,128)}, bf16[16,1024]{1,0:T(8,128)(2,1)}) custom-call(bf16[32,1024]{1,0:T(8,128)(2,1)S(1)} %get-tuple-element.12.refs_0_, f32[32,128]{1,0:T(8,128)S(1)} %get-tuple-element.13.refs_1_, f32[1,32]{1,0:T(1,128)S(1)} %get-tuple-element.14.refs_2_, ...), custom_call_target="tpu_custom_call" | custom-call | tf_op jit(solution)/shard_map/store_outputs/pallas_call | solution.py:396
